TPU v7x, 256 devices: a whole 4x4x8 slice. The times are simulated.
256 devices in a mesh: row: 16 (over x, z_hi, core), col: 16 (over y, z_lo).
Axes of the slice: x: 4, y: 4, z: 8 (z_hi: 2, z_lo: 4; z = z_hi * 4 + z_lo), core: 2. Of those that a mesh axis runs over, the one named last changes fastest.
Arguments:
- object_field: float32 [2, 6144, 6144], P(None, 'row', 'col'), may hold values from -6 to 6
- probe: float32 [2, 2, 256, 256], replicated, may hold values from -6 to 6
- patterns: float32 [16, 16, 6, 256, 256], P('row', 'col'), may hold values from 0.01 to 4
- positions: int32 [16, 16, 6, 2], P('row', 'col'), may hold values from -127 to 6015, as said below
- counts: int32 [16, 16], P('row', 'col'), may hold values from 1 to 6
Outputs:
- object_new: float32 [2, 6144, 6144], P(None, 'row', 'col')
- probe_new: float32 [2, 2, 256, 256], replicated
- position_step: float32 [16, 16, 6, 2], P('row', 'col')
Inputs may be any that keep to these rules, and one draw needn't show every extreme that they name: `positions`: the centre (top-left plus 256 // 2) of every slot's patch, live or not, lies inside the tile of the device that holds the slot, at least one pixel from the tile's first row and first column.
All inputs are finite; a program needn't handle non-finite values.
Results may differ from a plain program's by a relative error of at most 0.00018.
Values sent between devices are 32-bit elements; how exact they have to be, the bound alone decides.
A program may use at most 64 MiB of HBM per device.

v0:
```python
import functools

import jax
import jax.numpy as jnp
import ml_dtypes
import numpy as np
from jax import lax
from jax.experimental import pallas as pl
from jax.experimental.pallas import tpu as pltpu
from jax.sharding import PartitionSpec as P

MESH = pl.DeviceIdType.MESH
VMEM = pltpu.VMEM
f32 = jnp.float32
bf16 = jnp.bfloat16

WIN = 256
HALF = 128
TILE = 384
CAP = 6
EXT_ROWS = 8 + HALF + TILE + HALF + 8
OFFSETS = [(-1, 0), (1, 0), (0, -1), (0, 1), (-1, -1), (-1, 1), (1, -1), (1, 1)]


def dft_tables():
    k = np.arange(HALF)
    even = np.exp(-2j * np.pi * np.outer(2 * k, k) / WIN) / np.sqrt(WIN)
    odd = np.exp(-2j * np.pi * np.outer(2 * k + 1, k) / WIN) / np.sqrt(WIN)

    def block(z):
        return np.block([[z.real, -z.imag], [z.imag, z.real]])

    out = []
    for mat in (block(even), block(odd), block(even).T, block(odd).T):
        high = mat.astype(np.float32).astype(ml_dtypes.bfloat16)
        low = (mat - high.astype(np.float64)).astype(np.float32).astype(ml_dtypes.bfloat16)
        out += [high, low]
    return np.stack(out)


def order_table():
    table = np.zeros((WIN, WIN), np.float32)
    k = np.arange(HALF)
    table[2 * k, k] = 1
    table[2 * k + 1, HALF + k] = 1
    return table.astype(ml_dtypes.bfloat16)


def split(x):
    high = x.astype(bf16)
    return high, (x - high.astype(f32)).astype(bf16)


def mm(a, b):
    return jnp.dot(a, b, preferred_element_type=f32)


def neighbour(step):
    n_row, n_col = lax.axis_size("row"), lax.axis_size("col")
    r, c = lax.axis_index("row"), lax.axis_index("col")
    return (lax.rem(r + step[0] + n_row, n_row), lax.rem(c + step[1] + n_col, n_col))


def greet():
    barrier = pltpu.get_barrier_semaphore()
    for step in OFFSETS:
        pl.semaphore_signal(barrier, inc=1, device_id=neighbour(step), device_id_type=MESH)
    pl.semaphore_wait(barrier, len(OFFSETS))


def send_rows(d):
    return {-1: (136, 128), 0: (136, 384), 1: (392, 128)}[d]


def land_rows(d):
    return {-1: (520, 128), 0: (136, 384), 1: (8, 128)}[d]


def send_cols(d):
    return {-1: (1, 1), 0: (1, 3), 1: (3, 1)}[d]


def land_cols(d):
    return {-1: (4, 1), 0: (1, 3), 1: (0, 1)}[d]


def halo_kernel(obj, pats, meta, order, ext, spat, metas, turned, ssem, rsem, msend, mrecv):
    greet()
    for t in range(3):
        for ch in range(2):
            ext[ch, 1 + t, 136:520, :] = obj[ch, :, 128 * t : 128 * (t + 1)]
    metas[4] = meta[...]
    copies = []
    for i, (dr, dc) in enumerate(OFFSETS):
        r0, rn = send_rows(dr)
        q0, _ = land_rows(dr)
        c0, cn = send_cols(dc)
        e0, _ = land_cols(dc)
        copy = pltpu.make_async_remote_copy(
            src_ref=ext.at[:, pl.ds(c0, cn), pl.ds(r0, rn), :],
            dst_ref=ext.at[:, pl.ds(e0, cn), pl.ds(q0, rn), :],
            send_sem=ssem.at[i],
            recv_sem=rsem.at[i],
            device_id=neighbour((dr, dc)),
            device_id_type=MESH,
        )
        copy.start()
        copies.append(copy)
    for i, (dr, dc) in enumerate(OFFSETS):
        copy = pltpu.make_async_remote_copy(
            src_ref=metas.at[4],
            dst_ref=metas.at[(1 - dr) * 3 + 1 - dc],
            send_sem=msend.at[i],
            recv_sem=mrecv.at[i],
            device_id=neighbour((dr, dc)),
            device_id_type=MESH,
        )
        copy.start()
        copies.append(copy)

    def reorder(slot, _):
        high, low = split(jnp.sqrt(pats[slot]))
        sorted_cols = mm(high, order[...]) + mm(low, order[...])
        for j in range(2):
            turned[j] = sorted_cols[:, 128 * j : 128 * (j + 1)]
        for parity in range(2):
            for j in range(2):
                spat[slot, 128 * parity : 128 * (parity + 1), 128 * j : 128 * (j + 1)] = turned[
                    j, pl.ds(parity, 128, stride=2), :
                ]
        return 0

    lax.fori_loop(0, CAP, reorder, 0)
    for copy in copies:
        copy.wait()
    r, c = lax.axis_index("row"), lax.axis_index("col")
    for ch in range(2):
        for t in range(5):
            ext[ch, t, 0:8, :] = jnp.zeros((8, 128), f32)
            ext[ch, t, 648:656, :] = jnp.zeros((8, 128), f32)

    @pl.when(r == 0)
    def _():
        ext[:, :, 8:136, :] = jnp.zeros((2, 5, 128, 128), f32)

    @pl.when(r == lax.axis_size("row") - 1)
    def _():
        ext[:, :, 520:648, :] = jnp.zeros((2, 5, 128, 128), f32)

    @pl.when(c == 0)
    def _():
        ext[:, 0, 8:648, :] = jnp.zeros((2, 640, 128), f32)

    @pl.when(c == lax.axis_size("col") - 1)
    def _():
        ext[:, 4, 8:648, :] = jnp.zeros((2, 640, 128), f32)


def halo(obj, pats, meta, order):
    return pl.pallas_call(
        halo_kernel,
        out_shape=(
            jax.ShapeDtypeStruct((2, 5, EXT_ROWS, 128), f32),
            jax.ShapeDtypeStruct((CAP, WIN, WIN), f32),
            jax.ShapeDtypeStruct((9, 8, 128), jnp.int32),
        ),
        in_specs=[pl.BlockSpec(memory_space=VMEM)] * 4,
        out_specs=[pl.BlockSpec(memory_space=VMEM)] * 3,
        scratch_shapes=[
            VMEM((2, WIN, 128), f32),
            pltpu.SemaphoreType.DMA((8,)),
            pltpu.SemaphoreType.DMA((8,)),
            pltpu.SemaphoreType.DMA((8,)),
            pltpu.SemaphoreType.DMA((8,)),
        ],
        compiler_params=pltpu.CompilerParams(
            collective_id=0, has_side_effects=True, vmem_limit_bytes=40 * 2**20
        ),
        name="halo_in",
    )(obj, pats, meta, order)


def turn(x, shift):
    return pltpu.roll(x, shift, 1)


def slots_kernel(
    where,
    ext,
    probe,
    spat,
    tables,
    grad,
    weight,
    probe_out,
    raw,
    patch,
    slope,
    xs,
    ts,
    zs,
    rev,
    power,
    canvas,
    hg,
):
    r, c = lax.axis_index("row"), lax.axis_index("col")
    row_start, col_start = r * TILE, c * TILE
    lane = lax.broadcasted_iota(jnp.int32, (8, 128), 1)
    zero = jnp.zeros((8, 128), f32)

    def clear(ref, lead, rows):
        def step(i, _):
            for ix in lead:
                ref[(*ix, pl.ds(pl.multiple_of(i * 8, 8), 8), slice(None))] = zero
            return 0

        lax.fori_loop(0, rows // 8, step, 0)

    clear(grad, [(ch, t) for ch in range(2) for t in range(5)], EXT_ROWS)
    clear(canvas, [(t,) for t in range(8)], 904)
    clear(probe_out, [(i, t) for i in range(5) for t in range(2)], WIN)
    raw[...] = zero

    def fill_power(i, _):
        rows = pl.ds(pl.multiple_of(i * 8, 8), 8)
        for j in range(2):
            cols = slice(128 * j, 128 * (j + 1))
            power[j, rows, :] = (
                probe[0, 0, rows, cols] ** 2
                + probe[0, 1, rows, cols] ** 2
                + probe[1, 0, rows, cols] ** 2
                + probe[1, 1, rows, cols] ** 2
            )
        return 0

    lax.fori_loop(0, WIN // 8, fill_power, 0)

    for j in range(9):
        jr, jc = j // 3 - 1, j % 3 - 1
        inside = (r + jr >= 0) & (r + jr < lax.axis_size("row")) & (c + jc >= 0) & (c + jc < lax.axis_size("col"))
        live = jnp.where(inside, where[j, 0, 2 * CAP], 0)

        def place(slot, _, j=j):
            top = where[j, 0, 2 * slot] - row_start
            left = where[j, 0, 2 * slot + 1] - col_start

            @pl.when((top > -WIN) & (top < TILE) & (left > -WIN) & (left < TILE))
            def _():
                at = left + WIN
                tile, shift = at // 128, lax.rem(at, 128)
                keep = lane >= shift

                def rows_step(i, _):
                    src = pl.ds(pl.multiple_of(i * 8, 8), 8)
                    dst = pl.ds(top + WIN + i * 8, 8)
                    a, b = turn(power[0, src, :], shift), turn(power[1, src, :], shift)
                    canvas[tile, dst, :] += jnp.where(keep, a, 0.0)
                    canvas[tile + 1, dst, :] += jnp.where(keep, b, a)
                    canvas[tile + 2, dst, :] += jnp.where(keep, 0.0, b)
                    return 0

                lax.fori_loop(0, WIN // 8, rows_step, 0, unroll=4)

            return 0

        lax.fori_loop(0, live, place, 0)

    for t in range(3):
        weight[:, 128 * t : 128 * (t + 1)] = canvas[2 + t, pl.ds(WIN, TILE), :]

    def visit(slot, _):
        top = where[4, 0, 2 * slot] - row_start + HALF
        left = where[4, 0, 2 * slot + 1] - col_start + HALF

        base = left - 1
        tile, shift = base // 128, lax.rem(base, 128)
        last = jnp.minimum(tile + 3, 4)

        def take(i, _):
            src = pl.ds(top + i * 8, 8)
            dst = pl.ds(pl.multiple_of(i * 8, 8), 8)
            for ch in range(2):
                x = [ext[ch, tile, src, :], ext[ch, tile + 1, src, :], ext[ch, tile + 2, src, :], ext[ch, last, src, :]]
                got = []
                for more in range(3):
                    s = shift + more
                    back = lax.rem(256 - s, 128)
                    y = [turn(v, back) for v in x]
                    near = lane < 128 - s
                    over = lane < 256 - s
                    got.append(
                        [
                            jnp.where(near, y[j], jnp.where(over, y[j + 1], y[min(j + 2, 3)]))
                            for j in range(2)
                        ]
                    )
                for j in range(2):
                    patch[ch, j, dst, :] = got[1][j]
                    slope[ch, j, dst, :] = 0.5 * (got[2][j] - got[0][j])
            return 0

        lax.fori_loop(0, 34, take, 0, unroll=2)

        def leave(i, _):
            rows = [pl.multiple_of(i * 16 + 128 * h, 16) for h in range(2)]
            for j in range(2):
                cols = slice(128 * j, 128 * (j + 1))
                o = [[patch[ch, j, pl.ds(rw + 8, 16), :] for ch in range(2)] for rw in rows]
                for m in range(2):
                    e = []
                    for h in range(2):
                        pr = probe[m, 0, pl.ds(rows[h], 16), cols]
                        pi = probe[m, 1, pl.ds(rows[h], 16), cols]
                        e.append((pr * o[h][0] - pi * o[h][1], pr * o[h][1] + pi * o[h][0]))
                    for ch in range(2):
                        at = pl.ds(pl.multiple_of(i * 16 + 128 * ch, 16), 16)
                        for k, v in enumerate((e[0][ch] + e[1][ch], e[0][ch] - e[1][ch])):
                            high, low = split(v)
                            xs[m, 2 * k, at, cols] = high
                            xs[m, 2 * k + 1, at, cols] = low
            return 0

        lax.fori_loop(0, 8, leave, 0)

        def left_mm(k, high, low):
            return mm(tables[2 * k], high) + mm(tables[2 * k], low) + mm(tables[2 * k + 1], high)

        def right_mm(k, high, low):
            return mm(high, tables[2 * k]) + mm(low, tables[2 * k]) + mm(high, tables[2 * k + 1])

        for m in range(2):
            for k in range(2):
                y = left_mm(k, xs[m, 2 * k], xs[m, 2 * k + 1])
                for ch in range(2):
                    a, b = y[128 * ch : 128 * (ch + 1), :128], y[128 * ch : 128 * (ch + 1), 128:]
                    for q, v in enumerate((a + b, a - b)):
                        high, low = split(v)
                        at = (slice(128 * k, 128 * (k + 1)), slice(128 * ch, 128 * (ch + 1)))
                        ts[m, 2 * q, *at] = high
                        ts[m, 2 * q + 1, *at] = low
            for q in range(2):
                zs[m, q] = right_mm(2 + q, ts[m, 2 * q], ts[m, 2 * q + 1])

        def project(i, _):
            at = pl.ds(pl.multiple_of(i * 16, 16), 16)
            for q in range(2):
                z = [[zs[m, q, at, 128 * ch : 128 * (ch + 1)] for ch in range(2)] for m in range(2)]
                amp = z[0][0] ** 2 + z[0][1] ** 2 + z[1][0] ** 2 + z[1][1] ** 2
                factor = spat[slot, at, 128 * q : 128 * (q + 1)] * lax.rsqrt(jnp.maximum(amp, 0.0625))
                for m in range(2):
                    for ch in range(2):
                        high, low = split(z[m][ch] * factor)
                        ts[m, 2 * q, at, 128 * ch : 128 * (ch + 1)] = high
                        ts[m, 2 * q + 1, at, 128 * ch : 128 * (ch + 1)] = low
            return 0

        lax.fori_loop(0, 16, project, 0)

        for m in range(2):
            a = right_mm(0, ts[m, 0], ts[m, 1])
            b = right_mm(1, ts[m, 2], ts[m, 3])
            for half, v in enumerate((a + b, a - b)):
                high, low = split(v)
                for k in range(2):
                    for ch in range(2):
                        at = (slice(128 * ch, 128 * (ch + 1)), slice(128 * half, 128 * (half + 1)))
                        pick = (slice(128 * k, 128 * (k + 1)), slice(128 * ch, 128 * (ch + 1)))
                        xs[m, 2 * k, *at] = high[pick]
                        xs[m, 2 * k + 1, *at] = low[pick]
            u = left_mm(2, xs[m, 0], xs[m, 1])
            v = left_mm(3, xs[m, 2], xs[m, 3])
            for ch in range(2):
                at = slice(128 * ch, 128 * (ch + 1))
                rev[m, ch, 0:128, :] = u[at] + v[at]
                rev[m, ch, 128:256, :] = u[at] - v[at]

        hg[...] = jnp.zeros((4, 8, 128), f32)
        tile_g, shift_g = left // 128, lax.rem(left, 128)
        keep = lane >= shift_g

        def finish(i, _):
            at = pl.ds(pl.multiple_of(i * 8, 8), 8)
            dst = pl.ds(top + 8 + i * 8, 8)
            g = []
            acc = [zero] * 4
            for j in range(2):
                cols = slice(128 * j, 128 * (j + 1))
                o_re = patch[0, j, pl.ds(i * 8 + 8, 8), :]
                o_im = patch[1, j, pl.ds(i * 8 + 8, 8), :]
                w = power[j, at, :]
                g_re, g_im = -w * o_re, -w * o_im
                for m in range(2):
                    p_re, p_im = probe[m, 0, at, cols], probe[m, 1, at, cols]
                    v_re, v_im = rev[m, 0, at, cols], rev[m, 1, at, cols]
                    g_re += p_re * v_re + p_im * v_im
                    g_im += p_re * v_im - p_im * v_re
                    probe_out[2 * m, j, at, :] += o_re * v_re + o_im * v_im
                    probe_out[2 * m + 1, j, at, :] += o_re * v_im - o_im * v_re
                probe_out[4, j, at, :] += o_re * o_re + o_im * o_im
                d_re = 0.5 * (patch[0, j, pl.ds(i * 8 + 9, 8), :] - patch[0, j, pl.ds(i * 8 + 7, 8), :])
                d_im = 0.5 * (patch[1, j, pl.ds(i * 8 + 9, 8), :] - patch[1, j, pl.ds(i * 8 + 7, 8), :])
                s_re = slope[0, j, pl.ds(i * 8 + 8, 8), :]
                s_im = slope[1, j, pl.ds(i * 8 + 8, 8), :]
                acc[0] += g_re * d_re + g_im * d_im
                acc[1] += w * (d_re * d_re + d_im * d_im)
                acc[2] += g_re * s_re + g_im * s_im
                acc[3] += w * (s_re * s_re + s_im * s_im)
                g.append((g_re, g_im))
            for k in range(4):
                hg[k] += acc[k]
            for ch in range(2):
                a, b = turn(g[0][ch], shift_g), turn(g[1][ch], shift_g)
                grad[ch, tile_g, dst, :] += jnp.where(keep, a, 0.0)
                grad[ch, tile_g + 1, dst, :] += jnp.where(keep, b, a)
                grad[ch, tile_g + 2, dst, :] += jnp.where(keep, 0.0, b)
            return 0

        lax.fori_loop(0, WIN // 8, finish, 0, unroll=2)
        total = [jnp.sum(hg[k], axis=(0, 1), keepdims=True) for k in range(4)]
        at_row = lax.broadcasted_iota(jnp.int32, (8, 128), 0) == slot
        for k in range(2):
            value = total[2 * k] * lax.rsqrt(total[2 * k + 1] + 1e-6)
            raw[...] += jnp.where(at_row & (lane == k), value, 0.0)
        return 0

    lax.fori_loop(0, where[4, 0, 2 * CAP], visit, 0)


def slots(where, ext, probe, spat, tables):
    v = pl.BlockSpec(memory_space=VMEM)
    return pl.pallas_call(
        slots_kernel,
        out_shape=(
            jax.ShapeDtypeStruct((2, 5, EXT_ROWS, 128), f32),
            jax.ShapeDtypeStruct((TILE, TILE), f32),
            jax.ShapeDtypeStruct((5, 2, WIN, 128), f32),
            jax.ShapeDtypeStruct((8, 128), f32),
        ),
        in_specs=[pl.BlockSpec(memory_space=pltpu.SMEM), v, v, v, v],
        out_specs=[v, v, v, v],
        scratch_shapes=[
            VMEM((2, 2, 272, 128), f32),
            VMEM((2, 2, 272, 128), f32),
            VMEM((2, 4, WIN, WIN), bf16),
            VMEM((2, 4, WIN, WIN), bf16),
            VMEM((2, 2, WIN, WIN), f32),
            VMEM((2, 2, WIN, WIN), f32),
            VMEM((2, WIN, 128), f32),
            VMEM((8, 904, 128), f32),
            VMEM((4, 8, 128), f32),
        ],
        compiler_params=pltpu.CompilerParams(vmem_limit_bytes=50 * 2**20),
        name="slots",
    )(where, ext, probe, spat, tables)


def on_device(object_field, probe, patterns, positions, counts):
    meta = jnp.concatenate([positions.reshape(1, 2 * CAP), counts.reshape(1, 1)], axis=1)
    meta = jnp.pad(meta, ((0, 7), (0, 128 - 2 * CAP - 1)))
    ext, spat, where = halo(object_field, patterns[0, 0], meta, jnp.asarray(order_table()))
    grad, weight, probe_sum, raw = slots(where, ext, probe, spat, jnp.asarray(dft_tables()))
    return finish_all(object_field, probe, grad, weight, probe_sum, raw, counts)


def finish_all(object_field, probe, grad, weight, probe_sum, raw, counts):
    n_row, n_col = lax.axis_size("row"), lax.axis_size("col")

    def shifted(block, axis, distance):
        n = lax.axis_size(axis)
        route = [(i - distance, i) for i in range(n) if 0 <= i - distance < n]
        return lax.ppermute(block, axis, route)

    g = grad[:, :, 8:648, :].transpose(0, 2, 1, 3).reshape(2, 640, 640)
    from_above = shifted(g[:, 512:, :], "row", 1)
    from_below = shifted(g[:, :128, :], "row", -1)
    g = g.at[:, 128:256, :].add(from_above).at[:, 384:512, :].add(from_below)[:, 128:512, :]
    from_left = shifted(g[:, :, 512:], "col", 1)
    from_right = shifted(g[:, :, :128], "col", -1)
    g = g.at[:, :, 128:256].add(from_left).at[:, :, 384:512].add(from_right)[:, :, 128:512]
    power = jnp.max(jnp.sum(probe**2, axis=(0, 1)))
    object_new = object_field + g / (weight + 0.1 * power)[None]
    raw_all = raw[:CAP, :2]
    live = (jnp.arange(CAP) < counts[0, 0]).astype(f32)
    total, raw_total, count = lax.psum(
        (probe_sum, raw_all.sum(axis=0), counts[0, 0].astype(f32)), ("row", "col")
    )
    total = total.transpose(0, 2, 1, 3).reshape(5, WIN, WIN)
    wp = total[4]
    gp = total[:4].reshape(2, 2, WIN, WIN) - probe * wp
    probe_new = probe + gp / (wp + 0.1 * jnp.max(wp))
    step = ((raw_all - (raw_total / count)[None]) * live[:, None]).reshape(1, 1, CAP, 2)
    return object_new, probe_new, step


def solution(mesh):
    placed = (
        P(None, "row", "col"),
        P(),
        P("row", "col", None, None, None),
        P("row", "col", None, None),
        P("row", "col"),
    )
    return jax.shard_map(
        on_device,
        mesh=mesh,
        in_specs=placed,
        out_specs=(P(None, "row", "col"), P(), P("row", "col", None, None)),
        check_vma=False,
    )
```

profile of v0, /device:TPU:1, one launch (start us, length us, event | category | flops | bytes accessed | tf_op | source)
XLA Modules:
  0.0 447.9 jit_solution(9225151980270967954)
XLA Ops:
  7.9 0.8 copy.23
  8.9 1.3 copy-done.1
  10.2 1.4 copy-done.4
  11.6 0.9 copy-done.7
  12.5 59.3 %halo_in.1 = (f32[2,5,656,128]{3,2,1,0:T(8,128)S(1)}, f32[6,256,256]{2,1,0:T(8,128)S(1)}, s32[9,8,128]{2,1,0:T(8,128)S(1)}) custom-call(f32[2,384,384]{2,1,0:T(8,128)S(1)} %copy-done.1, f32[6,256,256]{2,1,0:T(8,128)S(1)} %bitcast.12, s32[8,128]{1,0:T(8,128)S(1)} %pad.12.meta, bf16[256,256]{1,0:T(8,128)(2,1)S(1)} %copy-done.7), custom_call_target="tpu_custom_call" | custom-call | tf_op jit(solution)/shard_map/halo_in/pallas_call | solution.py:160
  71.8 1.7 copy-done.3
  73.5 1.1 copy-done.5
  74.7 33.4 %slots.1 = (f32[2,5,656,128]{3,2,1,0:T(8,128)}, f32[384,384]{1,0:T(8,128)S(1)}, f32[5,2,256,128]{3,2,1,0:T(8,128)}, f32[8,128]{1,0:T(8,128)S(1)}) custom-call(s32[9,8,128]{2,1,0:T(8,128)S(1)} %get-tuple-element.58.where, f32[2,5,656,128]{3,2,1,0:T(8,128)} %copy-done.3, f32[2,2,256,256]{3,2,1,0:T(8,128)S(1)} %copy-done, f32[6,256,256]{2,1,0:T(8,128)} %copy-done.5, ...), custom_call_target="tpu_custom_call" | custom-call | tf_op jit(solution)/shard_map/slots/pallas_call | solution.py:432
  108.1 3.9 slice_bitcast_fusion
  112.0 4.6 %copy.24 = f32[2,640,5,128]{1,3,2,0:T(8,128)} copy(f32[2,640,5,128]{3,1,2,0:T(8,128)} %slice_bitcast_fusion) | data formatting | bytes 6553600 | tf_op jit(solution)/shard_map/transpose | solution.py:474
  116.6 1.2 slice.146
  117.8 11.9 %collective-permute-start = (f32[2,128,640]{1,2,0:T(8,128)S(1)}, f32[2,128,640]{1,2,0:T(8,128)}, u32[]{:S(2)}, u32[]{:S(2)}) collective-permute-start(f32[2,128,640]{1,2,0:T(8,128)S(1)} %slice.146), channel_id=1, source_target_pairs={{0,16},{16,32},{32,48},{48,64},{64,80},{80,96},{96,112},{112,128},... | collective-permute-start | bytes 1966088 | tf_op jit(solution)/shard_map/ppermute | solution.py:472
  129.8 95.3 %all-reduce.1 = (f32[2]{0:T(128)S(1)}, f32[]{:T(128)}) all-reduce(f32[2]{0:T(128)S(1)} %slice_reduce_fusion, f32[]{:T(128)S(6)} %convert_element_type.10), channel_id=1, replica_groups=mesh['row'=16,'col'=16] {'row','col'}, use_global_device_ids=true, to_apply=%region_5.6 | all-reduce | flops 3 | bytes 24 | tf_op jit(solution)/shard_map/psum | solution.py:485
  225.1 1.4 copy.26
  226.4 1.3 copy.30
  229.1 1.1 copy.25
  230.2 2.5 fusion.6
  232.7 2.8 collective-permute-start.1
  237.0 169.0 %all-reduce.4.cloned.1.call-done = f32[5,256,2,128]{3,1,2,0:T(8,128)} async-done(((f32[5,256,2,128]{3,1,2,0:T(8,128)}), f32[5,256,2,128]{3,1,2,0:T(8,128)}) %all-reduce.4.cloned.1.call-update) | async-done | bytes 1310736 | tf_op jit(solution)/shard_map/psum | solution.py:485
  406.0 1.7 fusion.7
  408.5 2.0 fusion.1
  410.5 2.2 fusion.5
  412.7 4.0 collective-permute-start.2
  416.7 0.7 broadcast_add_fusion.1
  417.4 1.3 copy.27
  418.8 1.3 collective-permute-start.3
  420.1 2.9 divide_add_fusion
  423.0 2.5 copy.33
  425.7 1.2 fusion.4
  426.8 11.6 %collective-permute-done.3 = f32[2,384,128]{1,2,0:T(8,128)} collective-permute-done((f32[2,384,128]{1,2,0:T(8,128)}, f32[2,384,128]{1,2,0:T(8,128)}, u32[]{:S(2)}, u32[]{:S(2)}) %collective-permute-start.3) | collective-permute-done | bytes 393248 | tf_op jit(solution)/shard_map/ppermute | solution.py:472
  438.4 1.1 fusion.3
  439.7 1.4 copy.32
  (38 shorter events, 2.9 us)
Async XLA Ops:
  7.2 67.5 %copy-start = (f32[2,2,256,256]{3,2,1,0:T(8,128)S(1)}, f32[2,2,256,256]{3,2,1,0:T(8,128)}, u32[]{:S(2)}) copy-start(f32[2,2,256,256]{3,2,1,0:T(8,128)} %probe.1) | copy-start | bytes 3145732
  7.2 398.9 %all-reduce.4.cloned.1.call-start = ((), (), s32[]{:S(2)}) async-start(), calls=%async_computation | async-start | bytes 2621440 | tf_op jit(solution)/shard_map/psum | solution.py:485
  8.9 1.3 copy-start.1
  10.2 1.4 copy-start.4
  11.6 0.9 copy-start.7
  12.5 62.2 %copy-start.6 = (bf16[8,256,256]{2,1,0:T(8,128)(2,1)S(1)}, bf16[8,256,256]{2,1,0:T(8,128)(2,1)}, u32[]{:S(2)}) copy-start(bf16[8,256,256]{2,1,0:T(8,128)(2,1)} %constant.121.clone.tables) | copy-start | bytes 3145732
  71.8 1.8 copy-start.3
  73.5 1.1 copy-start.5
  116.6 108.5 %copy-start.2 = (f32[2,384,384]{2,1,0:T(8,128)S(1)}, f32[2,384,384]{2,1,0:T(8,128)}, u32[]{:S(2)}) copy-start(f32[2,384,384]{2,1,0:T(8,128)} %obj.1) | copy-start | bytes 3538948
  117.8 112.4 %collective-permute-start = (f32[2,128,640]{1,2,0:T(8,128)S(1)}, f32[2,128,640]{1,2,0:T(8,128)}, u32[]{:S(2)}, u32[]{:S(2)}) collective-permute-start(f32[2,128,640]{1,2,0:T(8,128)S(1)} %slice.146), channel_id=1, source_target_pairs={{0,16},{16,32},{32,48},{48,64},{64,80},{80,96},{96,112},{112,128},... | collective-permute-start | bytes 1966088 | tf_op jit(solution)/shard_map/ppermute | solution.py:472
  232.7 175.8 %collective-permute-start.1 = (f32[2,128,640]{1,2,0:T(8,128)S(1)}, f32[2,128,640]{1,2,0:T(8,128)S(1)}, u32[]{:S(2)}, u32[]{:S(2)}) collective-permute-start(f32[2,128,640]{1,2,0:T(8,128)S(1)} %get-tuple-element.75), channel_id=1, source_target_pairs={{16,0},{32,16},{48,32},{64,48},{80,64},{96,80},{112,96},{128,112},... | collective-permute-start | bytes 1966088 | tf_op jit(solution)/shard_map/ppermute | solution.py:472
  410.5 6.9 %slice-start = ((f32[5,256,2,128]{3,1,2,0:T(8,128)}), f32[4,256,2,128]{3,1,2,0:T(8,128)S(1)}, s32[]{:S(2)}) async-start(f32[5,256,2,128]{3,1,2,0:T(8,128)} %all-reduce.4.cloned.1.call-done), calls=%async_computation.1 | async-start | bytes 2097152 | tf_op jit(solution)/shard_map/slice | solution.py:490
  412.7 12.9 %collective-permute-start.2 = (f32[2,384,128]{1,2,0:T(8,128)}, f32[2,384,128]{1,2,0:T(8,128)}, u32[]{:S(2)}, u32[]{:S(2)}) collective-permute-start(f32[2,384,128]{1,2,0:T(8,128)} %get-tuple-element.74), channel_id=1, source_target_pairs={{0,1},{1,2},{2,3},{3,4},{4,5},{5,6},{6,7},{7,8},{8,9},{9,10},{10,1... | collective-permute-start | bytes 1179656 | tf_op jit(solution)/shard_map/ppermute | solution.py:472
  418.8 19.7 %collective-permute-start.3 = (f32[2,384,128]{1,2,0:T(8,128)}, f32[2,384,128]{1,2,0:T(8,128)}, u32[]{:S(2)}, u32[]{:S(2)}) collective-permute-start(f32[2,384,128]{1,2,0:T(8,128)} %get-tuple-element.73), channel_id=1, source_target_pairs={{1,0},{2,1},{3,2},{4,3},{5,4},{6,5},{7,6},{8,7},{9,8},{10,9},{11,1... | collective-permute-start | bytes 1179656 | tf_op jit(solution)/shard_map/ppermute | solution.py:472
  420.1 5.4 %copy-start.8 = (f32[2,640,640]{1,2,0:T(8,128)S(1)}, f32[2,640,640]{1,2,0:T(8,128)}, u32[]{:S(2)}) copy-start(f32[2,640,640]{1,2,0:T(8,128)} %fusion.1) | copy-start | bytes 9830404
  425.6 13.9 %copy-start.9 = (f32[2,384,384]{1,2,0:T(8,128)S(1)}, f32[2,384,384]{1,2,0:T(8,128)}, u32[]{:S(2)}) copy-start(f32[2,384,384]{1,2,0:T(8,128)} %copy.26) | copy-start | bytes 3538948
  425.6 13.9 %copy-start.10 = (f32[384,384]{0,1:T(8,128)S(1)}, f32[384,384]{0,1:T(8,128)}, u32[]{:S(2)}) copy-start(f32[384,384]{0,1:T(8,128)} %copy.25) | copy-start | bytes 1769476
Sparse Core Ops, SparseCore 0:
  129.9 276.0 all-reduce.3
where the time goes:
time: 449 us; the launch traced here: 448 us
  waiting for transfers between devices  181 us (40%)
  blocking collectives  95.3 us (21%)
  Pallas kernels  92.7 us (21%)
  local copies, waits for them, and re-layouts  29.2 us (7%)
  starting transfers between devices  20.1 us (4%)
  between operations  16.1 us (4%)
  other arithmetic  13.9 us (3%)
    psum x1, waiting for transfers between devices, finish_all(): lax.psum((probe_sum, raw_all.sum(axis=0), counts[0, 0].astype(f32)), ('ro...  169 us
    psum x1, blocking collectives, finish_all(): lax.psum((probe_sum, raw_all.sum(axis=0), counts[0, 0].astype(f32)), ('ro...  95.3 us
    pallas_call x1, Pallas kernels, halo(): pl.pallas_call(halo_kernel, out_shape=(jax.ShapeDtypeStruct((2, 5, EXT_RO...  59.3 us
    pallas_call x1, Pallas kernels, slots(): pl.pallas_call(slots_kernel, out_shape=(jax.ShapeDtypeStruct((2, 5, EXT_R...  33.4 us
    ppermute x4, starting transfers between devices, shifted(): return lax.ppermute(block, axis, route)  20.1 us
    unnamed x27, local copies, waits for them, and re-layouts  13.9 us
    ppermute x4, waiting for transfers between devices, shifted(): return lax.ppermute(block, axis, route)  11.6 us
  transfers between devices with their start and end apart: 5, of which 2 were waited for; matrix products, arithmetic and copies ran while one was open for 4% of the time, Pallas kernels for 0%

commit v1 on v0

--- a/solution.py
+++ b/solution.py
@@ -220,7 +220,11 @@
     clear(grad, [(ch, t) for ch in range(2) for t in range(5)], EXT_ROWS)
     clear(canvas, [(t,) for t in range(8)], 904)
     clear(probe_out, [(i, t) for i in range(5) for t in range(2)], WIN)
-    raw[...] = zero
+    raw[...] = jnp.where(
+        (lax.broadcasted_iota(jnp.int32, (8, 128), 0) == 7) & (lane == 2),
+        where[4, 0, 2 * CAP].astype(f32),
+        0.0,
+    )
 
     def fill_power(i, _):
         rows = pl.ds(pl.multiple_of(i * 8, 8), 8)
@@ -455,42 +459,284 @@
     )(where, ext, probe, spat, tables)
 
 
+SHARDS = 32
+SHARD = 80
+PIECE = SHARD + 8
+
+
+def plane(dx, dy):
+    r, c = lax.axis_index("row"), lax.axis_index("col")
+    return (lax.rem(r + 4 * dx, 16), lax.rem(c + 4 * dy, 16))
+
+
+def depth_of():
+    r, c = lax.axis_index("row"), lax.axis_index("col")
+    return 4 * lax.rem(r // 2, 2) + lax.rem(c, 4)
+
+
+def along(dz):
+    r, c = lax.axis_index("row"), lax.axis_index("col")
+    z = lax.rem(depth_of() + dz, 8)
+    return (r // 4 * 4 + z // 4 * 2 + lax.rem(r, 2), c // 4 * 4 + lax.rem(z, 4))
+
+
+def sums_kernel(
+    grad,
+    weight,
+    obj,
+    probe,
+    part,
+    raw,
+    obj_new,
+    probe_new,
+    step,
+    strips,
+    sides,
+    corners,
+    mine,
+    mate_part,
+    plane_part,
+    deep,
+    deep_part,
+    deep_all,
+    all_sum,
+    flat,
+    hsend,
+    hrecv,
+    csend,
+    crecv,
+    psend,
+    precv,
+    zsend,
+    zrecv,
+):
+    r, c = lax.axis_index("row"), lax.axis_index("col")
+    core = lax.rem(r, 2)
+    own = r // 4 * 4 + c // 4
+    z = depth_of()
+    mate = (r + 1 - 2 * core, c)
+    planes = [(dx, dy) for dx in range(4) for dy in range(4) if (dx, dy) != (0, 0)]
+
+    barrier = pltpu.get_barrier_semaphore()
+    partners = [neighbour(s) for s in OFFSETS] + [mate]
+    partners += [plane(*p) for p in planes] + [along(d) for d in range(1, 8)]
+    for partner in partners:
+        pl.semaphore_signal(barrier, inc=1, device_id=partner, device_id_type=MESH)
+
+    def gather(i, _):
+        mine[i, 0:SHARD, :] = part[pl.ds(pl.multiple_of(i * SHARD, SHARD), SHARD), :]
+        mine[i, SHARD:PIECE, :] = raw[...]
+        return 0
+
+    lax.fori_loop(0, SHARDS, gather, 0)
+    pl.semaphore_wait(barrier, len(partners))
+
+    def send(src, dst, ssem, rsem, to):
+        copy = pltpu.make_async_remote_copy(
+            src_ref=src, dst_ref=dst, send_sem=ssem, recv_sem=rsem, device_id=to, device_id_type=MESH
+        )
+        copy.start()
+        return copy
+
+    half = SHARDS // 2
+    to_mate = send(
+        mine.at[pl.ds(half * (1 - core), half)], mate_part, csend.at[0], crecv.at[0], mate
+    )
+    halos = []
+    for i, (dr, dc) in enumerate(OFFSETS):
+        q0, qn = {-1: (8, 128), 0: (136, 384), 1: (520, 128)}[dr]
+        e0, en = {-1: (0, 1), 0: (1, 3), 1: (4, 1)}[dc]
+        src = grad.at[:, pl.ds(e0, en), pl.ds(q0, qn), :]
+        dst = strips.at[i] if i < 2 else sides.at[i - 2] if i < 4 else corners.at[i - 4]
+        halos.append(send(src, dst, hsend.at[i], hrecv.at[i], neighbour((dr, dc))))
+
+    to_mate.wait()
+
+    def add_mate(i, _):
+        mine[half * core + i] += mate_part[i]
+        return 0
+
+    lax.fori_loop(0, half, add_mate, 0)
+    copies = []
+    for i, (dx, dy) in enumerate(planes):
+        to = plane(dx, dy)
+        owner = to[0] // 4 * 4 + to[1] // 4
+        copies.append(
+            send(mine.at[half * core + owner], plane_part.at[i], psend.at[i], precv.at[i], to)
+        )
+    for copy in copies:
+        copy.wait()
+    total = mine[half * core + own]
+    for i in range(15):
+        total = total + plane_part[i]
+    deep[0:PIECE, :] = total
+    deep[PIECE:128, :] = jnp.zeros((128 - PIECE, 128), f32)
+    copies = []
+    for d in range(1, 8):
+        there = lax.rem(z + d, 8)
+        copies.append(
+            send(
+                deep.at[pl.ds(pl.multiple_of(there * 16, 16), 16)],
+                deep_part.at[d - 1],
+                zsend.at[d - 1],
+                zrecv.at[d - 1],
+                along(d),
+            )
+        )
+    for copy in copies:
+        copy.wait()
+    total = deep[pl.ds(pl.multiple_of(z * 16, 16), 16), :]
+    for d in range(7):
+        total = total + deep_part[d]
+    here = deep_all.at[pl.ds(pl.multiple_of(z * 16, 16), 16)]
+    deep_all[pl.ds(pl.multiple_of(z * 16, 16), 16), :] = total
+    copies = [send(here, here, zsend.at[6 + d], zrecv.at[6 + d], along(d)) for d in range(1, 8)]
+    for copy in copies:
+        copy.wait()
+    all_sum[half * core + own] = deep_all[0:PIECE, :]
+    block = all_sum.at[half * core + own]
+    copies = [
+        send(block, block, psend.at[15 + i], precv.at[15 + i], plane(*p)) for i, p in enumerate(planes)
+    ]
+    for copy in copies:
+        copy.wait()
+    block = all_sum.at[pl.ds(half * core, half)]
+    to_mate = send(block, block, csend.at[1], crecv.at[1], mate)
+
+    for copy in halos:
+        copy.wait()
+    n_row, n_col = lax.axis_size("row"), lax.axis_size("col")
+    row_ok = {-1: r < n_row - 1, 1: r > 0, 0: r >= 0}
+    col_ok = {-1: c < n_col - 1, 1: c > 0, 0: c >= 0}
+    ok = [row_ok[dr] & col_ok[dc] for dr, dc in OFFSETS]
+
+    def peak(i, top):
+        rows = pl.ds(pl.multiple_of(i * 8, 8), 8)
+        power = probe[0, 0, rows, :] ** 2 + probe[0, 1, rows, :] ** 2
+        power = power + probe[1, 0, rows, :] ** 2 + probe[1, 1, rows, :] ** 2
+        return jnp.maximum(top, power)
+
+    top = lax.fori_loop(0, WIN // 8, peak, jnp.zeros((8, WIN), f32))
+    floor = 0.1 * jnp.max(top, axis=(0, 1), keepdims=True)
+
+    for band in range(3):
+
+        def update(i, _, band=band):
+            rows = pl.ds(pl.multiple_of(band * 128 + i * 8, 8), 8)
+            thin = pl.ds(pl.multiple_of(i * 8, 8), 8)
+            for t in range(3):
+                cols = slice(128 * t, 128 * (t + 1))
+                down = weight[rows, cols] + floor
+                for ch in range(2):
+                    g = grad[ch, 1 + t, pl.ds(pl.multiple_of(136 + band * 128 + i * 8, 8), 8), :]
+                    for k, (dr, dc) in enumerate(OFFSETS):
+                        in_rows = dr == 0 or (dr == -1 and band == 2) or (dr == 1 and band == 0)
+                        in_cols = dc == 0 or (dc == -1 and t == 2) or (dc == 1 and t == 0)
+                        if not (in_rows and in_cols):
+                            continue
+                        if k < 2:
+                            v = strips[k, ch, t, thin, :]
+                        elif k < 4:
+                            v = sides[k - 2, ch, 0, rows, :]
+                        else:
+                            v = corners[k - 4, ch, 0, thin, :]
+                        g = g + jnp.where(ok[k], v, 0.0)
+                    obj_new[ch, rows, cols] = obj[ch, rows, cols] + g / down
+            return 0
+
+        lax.fori_loop(0, 16, update, 0)
+
+    to_mate.wait()
+
+    def spread(i, _):
+        flat[pl.ds(pl.multiple_of(i * SHARD, SHARD), SHARD), :] = all_sum[i, 0:SHARD, :]
+        return 0
+
+    lax.fori_loop(0, SHARDS, spread, 0)
+
+    def peak_sum(i, top):
+        return jnp.maximum(top, flat[pl.ds(pl.multiple_of(2048 + i * 8, 8), 8), :])
+
+    top = lax.fori_loop(0, 64, peak_sum, jnp.zeros((8, 128), f32))
+    floor_p = 0.1 * jnp.max(top, axis=(0, 1), keepdims=True)
+
+    def renew(i, _):
+        rows = pl.ds(pl.multiple_of(i * 8, 8), 8)
+        for j in range(2):
+            cols = slice(128 * j, 128 * (j + 1))
+
+            def at(k):
+                return flat[pl.ds(pl.multiple_of((2 * k + j) * WIN + i * 8, 8), 8), :]
+
+            wp = at(4)
+            scale = 1.0 / (wp + floor_p)
+            for m in range(2):
+                for ch in range(2):
+                    old = probe[m, ch, rows, cols]
+                    probe_new[m, ch, rows, cols] = old + (at(2 * m + ch) - old * wp) * scale
+        return 0
+
+    lax.fori_loop(0, WIN // 8, renew, 0)
+
+    rows8 = lax.broadcasted_iota(jnp.int32, (8, 128), 0)
+    lanes8 = lax.broadcasted_iota(jnp.int32, (8, 128), 1)
+    is_count = (rows8 == 7) & (lanes8 == 2)
+    sums = all_sum[0, SHARD:PIECE, :]
+    count = jnp.sum(jnp.where(is_count, sums, 0.0), axis=(0, 1), keepdims=True)
+    mine_count = jnp.sum(jnp.where(is_count, raw[...], 0.0), axis=(0, 1), keepdims=True)
+    mean = jnp.sum(sums, axis=0, keepdims=True) / count
+    step[...] = jnp.where(rows8.astype(f32) < mine_count, raw[...] - mean, 0.0)
+
+
+def sums(grad, weight, obj, probe, part, raw):
+    v = pl.BlockSpec(memory_space=VMEM)
+    dma = pltpu.SemaphoreType.DMA
+    return pl.pallas_call(
+        sums_kernel,
+        out_shape=(
+            jax.ShapeDtypeStruct((2, TILE, TILE), f32),
+            jax.ShapeDtypeStruct((2, 2, WIN, WIN), f32),
+            jax.ShapeDtypeStruct((8, 128), f32),
+        ),
+        in_specs=[v] * 6,
+        out_specs=[v] * 3,
+        scratch_shapes=[
+            VMEM((2, 2, 3, 128, 128), f32),
+            VMEM((2, 2, 1, TILE, 128), f32),
+            VMEM((4, 2, 1, 128, 128), f32),
+            VMEM((SHARDS, PIECE, 128), f32),
+            VMEM((SHARDS // 2, PIECE, 128), f32),
+            VMEM((15, PIECE, 128), f32),
+            VMEM((128, 128), f32),
+            VMEM((7, 16, 128), f32),
+            VMEM((128, 128), f32),
+            VMEM((SHARDS, PIECE, 128), f32),
+            VMEM((SHARDS * SHARD, 128), f32),
+            dma((8,)),
+            dma((8,)),
+            dma((2,)),
+            dma((2,)),
+            dma((30,)),
+            dma((30,)),
+            dma((14,)),
+            dma((14,)),
+        ],
+        compiler_params=pltpu.CompilerParams(
+            collective_id=1, has_side_effects=True, vmem_limit_bytes=50 * 2**20
+        ),
+        name="sums",
+    )(grad, weight, obj, probe, part, raw)
+
+
 def on_device(object_field, probe, patterns, positions, counts):
     meta = jnp.concatenate([positions.reshape(1, 2 * CAP), counts.reshape(1, 1)], axis=1)
     meta = jnp.pad(meta, ((0, 7), (0, 128 - 2 * CAP - 1)))
     ext, spat, where = halo(object_field, patterns[0, 0], meta, jnp.asarray(order_table()))
-    grad, weight, probe_sum, raw = slots(where, ext, probe, spat, jnp.asarray(dft_tables()))
-    return finish_all(object_field, probe, grad, weight, probe_sum, raw, counts)
-
-
-def finish_all(object_field, probe, grad, weight, probe_sum, raw, counts):
-    n_row, n_col = lax.axis_size("row"), lax.axis_size("col")
-
-    def shifted(block, axis, distance):
-        n = lax.axis_size(axis)
-        route = [(i - distance, i) for i in range(n) if 0 <= i - distance < n]
-        return lax.ppermute(block, axis, route)
-
-    g = grad[:, :, 8:648, :].transpose(0, 2, 1, 3).reshape(2, 640, 640)
-    from_above = shifted(g[:, 512:, :], "row", 1)
-    from_below = shifted(g[:, :128, :], "row", -1)
-    g = g.at[:, 128:256, :].add(from_above).at[:, 384:512, :].add(from_below)[:, 128:512, :]
-    from_left = shifted(g[:, :, 512:], "col", 1)
-    from_right = shifted(g[:, :, :128], "col", -1)
-    g = g.at[:, :, 128:256].add(from_left).at[:, :, 384:512].add(from_right)[:, :, 128:512]
-    power = jnp.max(jnp.sum(probe**2, axis=(0, 1)))
-    object_new = object_field + g / (weight + 0.1 * power)[None]
-    raw_all = raw[:CAP, :2]
-    live = (jnp.arange(CAP) < counts[0, 0]).astype(f32)
-    total, raw_total, count = lax.psum(
-        (probe_sum, raw_all.sum(axis=0), counts[0, 0].astype(f32)), ("row", "col")
+    grad, weight, part, raw = slots(where, ext, probe, spat, jnp.asarray(dft_tables()))
+    object_new, probe_new, step = sums(
+        grad, weight, object_field, probe, part.reshape(SHARDS * SHARD, 128), raw
     )
-    total = total.transpose(0, 2, 1, 3).reshape(5, WIN, WIN)
-    wp = total[4]
-    gp = total[:4].reshape(2, 2, WIN, WIN) - probe * wp
-    probe_new = probe + gp / (wp + 0.1 * jnp.max(wp))
-    step = ((raw_all - (raw_total / count)[None]) * live[:, None]).reshape(1, 1, CAP, 2)
-    return object_new, probe_new, step
+    return object_new, probe_new, step[:CAP, :2].reshape(1, 1, CAP, 2)
 
 
 def solution(mesh):

time: 449 us -> 207 us (0.46)
  waiting for transfers between devices: 181 us -> 0 us
  Pallas kernels: 92.7 us -> 194 us
  blocking collectives: 95.3 us -> 0 us
  starting transfers between devices: 20.1 us -> 0 us
  local copies, waits for them, and re-layouts: 29.2 us -> 11.1 us
  between operations: 16.1 us -> 1.31 us
  other arithmetic: 13.9 us -> 0.08 us
    psum x1 -> x0, waiting for transfers between devices: 169 us -> none  [finish_all(): lax.psum((probe_sum, raw_all.sum(axis=0), counts[0, 0].astype(f32)), ('ro...]
    psum x1 -> x0, blocking collectives: 95.3 us -> none  [finish_all(): lax.psum((probe_sum, raw_all.sum(axis=0), counts[0, 0].astype(f32)), ('ro...]
    pallas_call x0 -> x1, Pallas kernels: none -> 78.8 us  [sums(): pl.pallas_call(sums_kernel, out_shape=(jax.ShapeDtypeStruct((2, TILE, TIL...]
    pallas_call x1, Pallas kernels: 33.4 us -> 55.8 us  [slots(): pl.pallas_call(slots_kernel, out_shape=(jax.ShapeDtypeStruct((2, 5, EXT_R...]
    ppermute x4 -> x0, starting transfers between devices: 20.1 us -> none  [shifted(): return lax.ppermute(block, axis, route)]
    ppermute x4 -> x0, waiting for transfers between devices: 11.6 us -> none  [shifted(): return lax.ppermute(block, axis, route)]
    transpose x2 -> x0, local copies, waits for them, and re-layouts: 8.49 us -> none  [finish_all(): g = grad[:, :, 8:648, :].transpose(0, 2, 1, 3).reshape(2, 640, 640)]
    unnamed x27 -> x19, local copies, waits for them, and re-layouts: 13.9 us -> 10.3 us
  transfers between devices with their start and end apart: 5 -> 0, of which waited for: 2 -> 0; matrix products, arithmetic and copies ran while one was open for 4% -> 0% of each run, Pallas kernels for 0% -> 0%
where the time goes in v1:
time: 207 us; the launch traced here: 206 us
  Pallas kernels  194 us (94%)
  local copies, waits for them, and re-layouts  11.1 us (5%)
    pallas_call x1, Pallas kernels, sums(): pl.pallas_call(sums_kernel, out_shape=(jax.ShapeDtypeStruct((2, TILE, TIL...  78.8 us
    pallas_call x1, Pallas kernels, halo(): pl.pallas_call(halo_kernel, out_shape=(jax.ShapeDtypeStruct((2, 5, EXT_RO...  59.3 us
    pallas_call x1, Pallas kernels, slots(): pl.pallas_call(slots_kernel, out_shape=(jax.ShapeDtypeStruct((2, 5, EXT_R...  55.8 us
    unnamed x19, local copies, waits for them, and re-layouts  10.3 us

profile of v1, /device:TPU:1, one launch (start us, length us, event | category | flops | bytes accessed | tf_op | source)
XLA Modules:
  0.0 206.4 jit_solution(3598136803781790426)
XLA Ops:
  1.3 0.8 copy.12
  2.0 0.1 reshape.15
  2.1 0.1 pad_add_fusion
  2.2 0.0 copy-start
  2.2 1.3 copy-done
  3.5 0.0 copy-start.3
  3.5 1.4 copy-done.3
  4.9 0.0 copy-start.7
  4.9 0.9 copy-done.7
  5.8 0.0 copy-start.1
  5.8 0.0 copy-start.6
  5.8 59.3 %halo_in.1 = (f32[2,5,656,128]{3,2,1,0:T(8,128)S(1)}, f32[6,256,256]{2,1,0:T(8,128)S(1)}, s32[9,8,128]{2,1,0:T(8,128)S(1)}) custom-call(f32[2,384,384]{2,1,0:T(8,128)S(1)} %copy-done, f32[6,256,256]{2,1,0:T(8,128)S(1)} %bitcast.4, s32[8,128]{1,0:T(8,128)S(1)} %pad.4.meta, bf16[256,256]{1,0:T(8,128)(2,1)S(1)} %copy-done.7), custom_call_target="tpu_custom_call" | custom-call | tf_op jit(solution)/shard_map/halo_in/pallas_call | solution.py:160
  65.1 0.0 copy-start.2
  65.1 1.8 copy-done.2
  66.9 0.0 copy-start.4
  66.9 1.1 copy-done.4
  68.0 0.0 copy-done.1
  68.0 0.0 copy-done.6
  68.0 55.8 %slots.1 = (f32[2,5,656,128]{3,2,1,0:T(8,128)}, f32[384,384]{1,0:T(8,128)S(1)}, f32[5,2,256,128]{3,2,1,0:T(8,128)S(1)}, f32[8,128]{1,0:T(8,128)S(1)}) custom-call(s32[9,8,128]{2,1,0:T(8,128)S(1)} %get-tuple-element.13.where, f32[2,5,656,128]{3,2,1,0:T(8,128)} %copy-done.2, f32[2,2,256,256]{3,2,1,0:T(8,128)S(1)} %copy-done.1, f32[6,256,256]{2,1,0:T(8,128)} %copy-done.4, ...), custom_call_target="tpu_custom_call" | custom-call | tf_op jit(solution)/shard_map/slots/pallas_call | solution.py:436
  123.9 0.0 copy-start.5
  123.9 1.1 copy-done.5
  125.0 78.8 %sums.1 = (f32[2,384,384]{2,1,0:T(8,128)S(1)}, f32[2,2,256,256]{3,2,1,0:T(8,128)S(1)}, f32[8,128]{1,0:T(8,128)S(1)}) custom-call(f32[2,5,656,128]{3,2,1,0:T(8,128)} %get-tuple-element.16.grad, f32[384,384]{1,0:T(8,128)S(1)} %get-tuple-element.17.weight, f32[2,384,384]{2,1,0:T(8,128)} %obj.3, f32[2,2,256,256]{3,2,1,0:T(8,128)S(1)} %copy-done.1, ...), custom_call_target="tpu_custom_call" | custom-call | tf_op jit(solution)/shard_map/sums/pallas_call | solution.py:694
  203.8 0.6 copy.13
  204.4 1.0 copy.17
  205.5 1.0 copy.18
  (1 shorter events, 0.0 us)
Async XLA Ops:
  2.2 1.3 copy-start
  3.5 1.4 copy-start.3
  4.9 0.9 copy-start.7
  5.8 62.2 %copy-start.1 = (f32[2,2,256,256]{3,2,1,0:T(8,128)S(1)}, f32[2,2,256,256]{3,2,1,0:T(8,128)}, u32[]{:S(2)}) copy-start(f32[2,2,256,256]{3,2,1,0:T(8,128)} %probe.3) | copy-start | bytes 3145732
  5.8 62.2 %copy-start.6 = (bf16[8,256,256]{2,1,0:T(8,128)(2,1)S(1)}, bf16[8,256,256]{2,1,0:T(8,128)(2,1)}, u32[]{:S(2)}) copy-start(bf16[8,256,256]{2,1,0:T(8,128)(2,1)} %constant.7.clone.tables) | copy-start | bytes 3145732
  65.1 1.8 copy-start.2
  66.9 1.2 copy-start.4
  123.9 1.1 copy-start.5

commit v2 on v1

--- a/solution.py
+++ b/solution.py
@@ -18,6 +18,7 @@
 HALF = 128
 TILE = 384
 CAP = 6
+STEP = 32
 EXT_ROWS = 8 + HALF + TILE + HALF + 8
 OFFSETS = [(-1, 0), (1, 0), (0, -1), (0, 1), (-1, -1), (-1, 1), (1, -1), (1, 1)]
 
@@ -68,55 +69,39 @@
     pl.semaphore_wait(barrier, len(OFFSETS))
 
 
-def send_rows(d):
-    return {-1: (136, 128), 0: (136, 384), 1: (392, 128)}[d]
-
-
-def land_rows(d):
-    return {-1: (520, 128), 0: (136, 384), 1: (8, 128)}[d]
-
-
-def send_cols(d):
-    return {-1: (1, 1), 0: (1, 3), 1: (3, 1)}[d]
-
-
-def land_cols(d):
-    return {-1: (4, 1), 0: (1, 3), 1: (0, 1)}[d]
+def send(src, dst, ssem, rsem, to):
+    copy = pltpu.make_async_remote_copy(
+        src_ref=src, dst_ref=dst, send_sem=ssem, recv_sem=rsem, device_id=to, device_id_type=MESH
+    )
+    copy.start()
+    return copy
 
 
 def halo_kernel(obj, pats, meta, order, ext, spat, metas, turned, ssem, rsem, msend, mrecv):
+    core = lax.rem(lax.axis_index("row"), 2)
     greet()
     for t in range(3):
         for ch in range(2):
             ext[ch, 1 + t, 136:520, :] = obj[ch, :, 128 * t : 128 * (t + 1)]
     metas[4] = meta[...]
-    copies = []
-    for i, (dr, dc) in enumerate(OFFSETS):
-        r0, rn = send_rows(dr)
-        q0, _ = land_rows(dr)
-        c0, cn = send_cols(dc)
-        e0, _ = land_cols(dc)
-        copy = pltpu.make_async_remote_copy(
-            src_ref=ext.at[:, pl.ds(c0, cn), pl.ds(r0, rn), :],
-            dst_ref=ext.at[:, pl.ds(e0, cn), pl.ds(q0, rn), :],
-            send_sem=ssem.at[i],
-            recv_sem=rsem.at[i],
-            device_id=neighbour((dr, dc)),
-            device_id_type=MESH,
+
+    def strip(tile, tiles, row, rows):
+        return ext.at[:, pl.ds(tile, tiles), pl.ds(row, rows), :]
+
+    tops = [
+        send(strip(1, 3, 136, 128), strip(1, 3, 520, 128), ssem.at[0], rsem.at[0], neighbour((-1, 0))),
+        send(strip(1, 3, 392, 128), strip(1, 3, 8, 128), ssem.at[1], rsem.at[1], neighbour((1, 0))),
+    ]
+    small = [
+        send(
+            metas.at[4],
+            metas.at[(1 - dr) * 3 + 1 - dc],
+            msend.at[i],
+            mrecv.at[i],
+            neighbour((dr, dc)),
         )
-        copy.start()
-        copies.append(copy)
-    for i, (dr, dc) in enumerate(OFFSETS):
-        copy = pltpu.make_async_remote_copy(
-            src_ref=metas.at[4],
-            dst_ref=metas.at[(1 - dr) * 3 + 1 - dc],
-            send_sem=msend.at[i],
-            recv_sem=mrecv.at[i],
-            device_id=neighbour((dr, dc)),
-            device_id_type=MESH,
-        )
-        copy.start()
-        copies.append(copy)
+        for i, (dr, dc) in enumerate(OFFSETS)
+    ]
 
     def reorder(slot, _):
         high, low = split(jnp.sqrt(pats[slot]))
@@ -131,7 +116,26 @@
         return 0
 
     lax.fori_loop(0, CAP, reorder, 0)
-    for copy in copies:
+    for copy in tops:
+        copy.wait()
+    outer = pl.multiple_of(8 + 512 * core, 8)
+    left, right = neighbour((0, -1)), neighbour((0, 1))
+    far = [
+        send(strip(1, 1, outer, 128), strip(4, 1, outer, 128), ssem.at[2], rsem.at[2], left),
+        send(strip(3, 1, outer, 128), strip(0, 1, outer, 128), ssem.at[3], rsem.at[3], right),
+    ]
+    sides = [
+        send(strip(1, 1, 136, 384), strip(4, 1, 136, 384), ssem.at[4], rsem.at[4], left),
+        send(strip(3, 1, 136, 384), strip(0, 1, 136, 384), ssem.at[5], rsem.at[5], right),
+    ]
+    mate = (lax.axis_index("row") + 1 - 2 * core, lax.axis_index("col"))
+    near = pl.multiple_of(392 - 256 * core, 8)
+    for k, tile in enumerate((4, 0)):
+        sides[k].wait()
+        far.append(
+            send(strip(tile, 1, near, 128), strip(tile, 1, outer, 128), ssem.at[6 + k], rsem.at[6 + k], mate)
+        )
+    for copy in far + small:
         copy.wait()
     r, c = lax.axis_index("row"), lax.axis_index("col")
     for ch in range(2):
@@ -174,7 +178,7 @@
             pltpu.SemaphoreType.DMA((8,)),
         ],
         compiler_params=pltpu.CompilerParams(
-            collective_id=0, has_side_effects=True, vmem_limit_bytes=40 * 2**20
+            collective_id=0, has_side_effects=True, vmem_limit_bytes=20 * 2**20
         ),
         name="halo_in",
     )(obj, pats, meta, order)
@@ -202,7 +206,6 @@
     rev,
     power,
     canvas,
-    hg,
 ):
     r, c = lax.axis_index("row"), lax.axis_index("col")
     row_start, col_start = r * TILE, c * TILE
@@ -215,11 +218,12 @@
                 ref[(*ix, pl.ds(pl.multiple_of(i * 8, 8), 8), slice(None))] = zero
             return 0
 
-        lax.fori_loop(0, rows // 8, step, 0)
+        lax.fori_loop(0, rows // 8, step, 0, unroll=2)
 
     clear(grad, [(ch, t) for ch in range(2) for t in range(5)], EXT_ROWS)
-    clear(canvas, [(t,) for t in range(8)], 904)
     clear(probe_out, [(i, t) for i in range(5) for t in range(2)], WIN)
+    for t in range(3):
+        canvas[2 + t, WIN : WIN + TILE, :] = jnp.zeros((TILE, 128), f32)
     raw[...] = jnp.where(
         (lax.broadcasted_iota(jnp.int32, (8, 128), 0) == 7) & (lane == 2),
         where[4, 0, 2 * CAP].astype(f32),
@@ -238,7 +242,7 @@
             )
         return 0
 
-    lax.fori_loop(0, WIN // 8, fill_power, 0)
+    lax.fori_loop(0, WIN // 8, fill_power, 0, unroll=4)
 
     for j in range(9):
         jr, jc = j // 3 - 1, j % 3 - 1
@@ -253,18 +257,18 @@
             def _():
                 at = left + WIN
                 tile, shift = at // 128, lax.rem(at, 128)
-                keep = lane >= shift
+                keep = lax.broadcasted_iota(jnp.int32, (32, 128), 1) >= shift
 
                 def rows_step(i, _):
-                    src = pl.ds(pl.multiple_of(i * 8, 8), 8)
-                    dst = pl.ds(top + WIN + i * 8, 8)
+                    src = pl.ds(pl.multiple_of(i * 32, 32), 32)
+                    dst = pl.ds(top + WIN + i * 32, 32)
                     a, b = turn(power[0, src, :], shift), turn(power[1, src, :], shift)
                     canvas[tile, dst, :] += jnp.where(keep, a, 0.0)
                     canvas[tile + 1, dst, :] += jnp.where(keep, b, a)
                     canvas[tile + 2, dst, :] += jnp.where(keep, 0.0, b)
                     return 0
 
-                lax.fori_loop(0, WIN // 8, rows_step, 0, unroll=4)
+                lax.fori_loop(jnp.maximum(-top, 0) // 32, (jnp.minimum(TILE - top, WIN) + 31) // 32, rows_step, 0)
 
             return 0
 
@@ -280,31 +284,19 @@
         base = left - 1
         tile, shift = base // 128, lax.rem(base, 128)
         last = jnp.minimum(tile + 3, 4)
-
-        def take(i, _):
-            src = pl.ds(top + i * 8, 8)
-            dst = pl.ds(pl.multiple_of(i * 8, 8), 8)
-            for ch in range(2):
-                x = [ext[ch, tile, src, :], ext[ch, tile + 1, src, :], ext[ch, tile + 2, src, :], ext[ch, last, src, :]]
-                got = []
-                for more in range(3):
-                    s = shift + more
-                    back = lax.rem(256 - s, 128)
-                    y = [turn(v, back) for v in x]
-                    near = lane < 128 - s
-                    over = lane < 256 - s
-                    got.append(
-                        [
-                            jnp.where(near, y[j], jnp.where(over, y[j + 1], y[min(j + 2, 3)]))
-                            for j in range(2)
-                        ]
-                    )
-                for j in range(2):
-                    patch[ch, j, dst, :] = got[1][j]
-                    slope[ch, j, dst, :] = 0.5 * (got[2][j] - got[0][j])
-            return 0
-
-        lax.fori_loop(0, 34, take, 0, unroll=2)
+        apart = lax.broadcasted_iota(jnp.int32, (512, 256), 0) - lax.broadcasted_iota(
+            jnp.int32, (512, 256), 1
+        )
+        move = jnp.where(apart == shift + 1, 1.0, 0.0).astype(bf16)
+        differ = jnp.where(apart == shift + 2, 0.5, jnp.where(apart == shift, -0.5, 0.0)).astype(bf16)
+        shifter = jnp.concatenate([move, differ], axis=1)
+        for ch in range(2):
+            x = [ext[ch, t, pl.ds(top, 272), :] for t in (tile, tile + 1, tile + 2, last)]
+            high, low = split(jnp.concatenate(x, axis=1))
+            y = mm(high, shifter) + mm(low, shifter)
+            for j in range(2):
+                patch[ch, j] = y[:, 128 * j : 128 * (j + 1)]
+                slope[ch, j] = y[:, 256 + 128 * j : 256 + 128 * (j + 1)]
 
         def leave(i, _):
             rows = [pl.multiple_of(i * 16 + 128 * h, 16) for h in range(2)]
@@ -325,7 +317,7 @@
                             xs[m, 2 * k + 1, at, cols] = low
             return 0
 
-        lax.fori_loop(0, 8, leave, 0)
+        lax.fori_loop(0, 8, leave, 0, unroll=True)
 
         def left_mm(k, high, low):
             return mm(tables[2 * k], high) + mm(tables[2 * k], low) + mm(tables[2 * k + 1], high)
@@ -359,7 +351,7 @@
                         ts[m, 2 * q + 1, at, 128 * ch : 128 * (ch + 1)] = low
             return 0
 
-        lax.fori_loop(0, 16, project, 0)
+        lax.fori_loop(0, 16, project, 0, unroll=True)
 
         for m in range(2):
             a = right_mm(0, ts[m, 0], ts[m, 1])
@@ -379,19 +371,21 @@
                 rev[m, ch, 0:128, :] = u[at] + v[at]
                 rev[m, ch, 128:256, :] = u[at] - v[at]
 
-        hg[...] = jnp.zeros((4, 8, 128), f32)
         tile_g, shift_g = left // 128, lax.rem(left, 128)
-        keep = lane >= shift_g
-
-        def finish(i, _):
-            at = pl.ds(pl.multiple_of(i * 8, 8), 8)
-            dst = pl.ds(top + 8 + i * 8, 8)
+        keep = lax.broadcasted_iota(jnp.int32, (STEP, 128), 1) >= shift_g
+
+        def fold(x):
+            return sum(x[8 * k : 8 * (k + 1)] for k in range(STEP // 8))
+
+        def finish(i, acc):
+            at = pl.ds(pl.multiple_of(i * STEP, STEP), STEP)
+            dst = pl.ds(top + 8 + i * STEP, STEP)
             g = []
-            acc = [zero] * 4
+            acc = list(acc)
             for j in range(2):
                 cols = slice(128 * j, 128 * (j + 1))
-                o_re = patch[0, j, pl.ds(i * 8 + 8, 8), :]
-                o_im = patch[1, j, pl.ds(i * 8 + 8, 8), :]
+                o_re = patch[0, j, pl.ds(i * STEP + 8, STEP), :]
+                o_im = patch[1, j, pl.ds(i * STEP + 8, STEP), :]
                 w = power[j, at, :]
                 g_re, g_im = -w * o_re, -w * o_im
                 for m in range(2):
@@ -402,26 +396,28 @@
                     probe_out[2 * m, j, at, :] += o_re * v_re + o_im * v_im
                     probe_out[2 * m + 1, j, at, :] += o_re * v_im - o_im * v_re
                 probe_out[4, j, at, :] += o_re * o_re + o_im * o_im
-                d_re = 0.5 * (patch[0, j, pl.ds(i * 8 + 9, 8), :] - patch[0, j, pl.ds(i * 8 + 7, 8), :])
-                d_im = 0.5 * (patch[1, j, pl.ds(i * 8 + 9, 8), :] - patch[1, j, pl.ds(i * 8 + 7, 8), :])
-                s_re = slope[0, j, pl.ds(i * 8 + 8, 8), :]
-                s_im = slope[1, j, pl.ds(i * 8 + 8, 8), :]
-                acc[0] += g_re * d_re + g_im * d_im
-                acc[1] += w * (d_re * d_re + d_im * d_im)
-                acc[2] += g_re * s_re + g_im * s_im
-                acc[3] += w * (s_re * s_re + s_im * s_im)
+                d_re = 0.5 * (
+                    patch[0, j, pl.ds(i * STEP + 9, STEP), :] - patch[0, j, pl.ds(i * STEP + 7, STEP), :]
+                )
+                d_im = 0.5 * (
+                    patch[1, j, pl.ds(i * STEP + 9, STEP), :] - patch[1, j, pl.ds(i * STEP + 7, STEP), :]
+                )
+                s_re = slope[0, j, pl.ds(i * STEP + 8, STEP), :]
+                s_im = slope[1, j, pl.ds(i * STEP + 8, STEP), :]
+                acc[0] += fold(g_re * d_re + g_im * d_im)
+                acc[1] += fold(w * (d_re * d_re + d_im * d_im))
+                acc[2] += fold(g_re * s_re + g_im * s_im)
+                acc[3] += fold(w * (s_re * s_re + s_im * s_im))
                 g.append((g_re, g_im))
-            for k in range(4):
-                hg[k] += acc[k]
             for ch in range(2):
                 a, b = turn(g[0][ch], shift_g), turn(g[1][ch], shift_g)
                 grad[ch, tile_g, dst, :] += jnp.where(keep, a, 0.0)
                 grad[ch, tile_g + 1, dst, :] += jnp.where(keep, b, a)
                 grad[ch, tile_g + 2, dst, :] += jnp.where(keep, 0.0, b)
-            return 0
-
-        lax.fori_loop(0, WIN // 8, finish, 0, unroll=2)
-        total = [jnp.sum(hg[k], axis=(0, 1), keepdims=True) for k in range(4)]
+            return tuple(acc)
+
+        acc = lax.fori_loop(0, WIN // STEP, finish, (zero,) * 4, unroll=2)
+        total = [jnp.sum(acc[k], axis=(0, 1), keepdims=True) for k in range(4)]
         at_row = lax.broadcasted_iota(jnp.int32, (8, 128), 0) == slot
         for k in range(2):
             value = total[2 * k] * lax.rsqrt(total[2 * k + 1] + 1e-6)
@@ -452,9 +448,8 @@
             VMEM((2, 2, WIN, WIN), f32),
             VMEM((2, WIN, 128), f32),
             VMEM((8, 904, 128), f32),
-            VMEM((4, 8, 128), f32),
         ],
-        compiler_params=pltpu.CompilerParams(vmem_limit_bytes=50 * 2**20),
+        compiler_params=pltpu.CompilerParams(vmem_limit_bytes=24 * 2**20),
         name="slots",
     )(where, ext, probe, spat, tables)
 
@@ -490,9 +485,12 @@
     obj_new,
     probe_new,
     step,
-    strips,
-    sides,
-    corners,
+    mate_rows,
+    corner_in,
+    row_out,
+    row_in,
+    side_out,
+    side_in,
     mine,
     mate_part,
     plane_part,
@@ -511,14 +509,17 @@
     zrecv,
 ):
     r, c = lax.axis_index("row"), lax.axis_index("col")
+    n_row, n_col = lax.axis_size("row"), lax.axis_size("col")
     core = lax.rem(r, 2)
     own = r // 4 * 4 + c // 4
     z = depth_of()
     mate = (r + 1 - 2 * core, c)
+    beyond = (lax.rem(r - 1 + 2 * core + n_row, n_row), c)
+    left, right = neighbour((0, -1)), neighbour((0, 1))
     planes = [(dx, dy) for dx in range(4) for dy in range(4) if (dx, dy) != (0, 0)]
 
     barrier = pltpu.get_barrier_semaphore()
-    partners = [neighbour(s) for s in OFFSETS] + [mate]
+    partners = [left, right, mate, beyond]
     partners += [plane(*p) for p in planes] + [along(d) for d in range(1, 8)]
     for partner in partners:
         pl.semaphore_signal(barrier, inc=1, device_id=partner, device_id_type=MESH)
@@ -531,25 +532,39 @@
     lax.fori_loop(0, SHARDS, gather, 0)
     pl.semaphore_wait(barrier, len(partners))
 
-    def send(src, dst, ssem, rsem, to):
-        copy = pltpu.make_async_remote_copy(
-            src_ref=src, dst_ref=dst, send_sem=ssem, recv_sem=rsem, device_id=to, device_id_type=MESH
-        )
-        copy.start()
-        return copy
-
+    outer_from = pl.multiple_of(8 + 512 * core, 8)
+    inner_from = pl.multiple_of(520 - 512 * core, 8)
+    outer_to = pl.multiple_of(256 * core, 8)
+    inner_to = pl.multiple_of(256 - 256 * core, 8)
+    col_ok = [c > 0, c < n_col - 1]
+    outer_ok = jnp.where(core == 0, r, n_row - 1 - r) > 0
+
+    rows_to_mate = send(
+        grad.at[:, :, pl.ds(inner_from, 128), :], mate_rows, csend.at[2], crecv.at[2], mate
+    )
     half = SHARDS // 2
     to_mate = send(
         mine.at[pl.ds(half * (1 - core), half)], mate_part, csend.at[0], crecv.at[0], mate
     )
-    halos = []
-    for i, (dr, dc) in enumerate(OFFSETS):
-        q0, qn = {-1: (8, 128), 0: (136, 384), 1: (520, 128)}[dr]
-        e0, en = {-1: (0, 1), 0: (1, 3), 1: (4, 1)}[dc]
-        src = grad.at[:, pl.ds(e0, en), pl.ds(q0, qn), :]
-        dst = strips.at[i] if i < 2 else sides.at[i - 2] if i < 4 else corners.at[i - 4]
-        halos.append(send(src, dst, hsend.at[i], hrecv.at[i], neighbour((dr, dc))))
-
+    edge = pl.ds(outer_from, 128)
+    corners = [
+        send(grad.at[:, 4, edge, :], corner_in.at[0], hsend.at[0], hrecv.at[0], right),
+        send(grad.at[:, 0, edge, :], corner_in.at[1], hsend.at[1], hrecv.at[1], left),
+    ]
+
+    rows_to_mate.wait()
+    for k, tile in enumerate((4, 0)):
+        for ch in range(2):
+            side_out[k, ch] = grad[ch, tile, 136:520, :]
+            side_out[k, ch, pl.ds(inner_to, 128), :] += mate_rows[ch, tile]
+
+    def send_sides(ch):
+        return [
+            send(side_out.at[k, ch], side_in.at[k, ch], hsend.at[2 + 2 * k + ch], hrecv.at[2 + 2 * k + ch], to)
+            for k, to in enumerate((right, left))
+        ]
+
+    sides = send_sides(0)
     to_mate.wait()
 
     def add_mate(i, _):
@@ -564,6 +579,16 @@
         copies.append(
             send(mine.at[half * core + owner], plane_part.at[i], psend.at[i], precv.at[i], to)
         )
+    for copy in corners:
+        copy.wait()
+    for ch in range(2):
+        for t in range(3):
+            v = grad[ch, 1 + t, edge, :]
+            if t == 0:
+                v = v + jnp.where(col_ok[0], corner_in[0, ch], 0.0)
+            if t == 2:
+                v = v + jnp.where(col_ok[1], corner_in[1, ch], 0.0)
+            row_out[ch, t] = v
     for copy in copies:
         copy.wait()
     total = mine[half * core + own]
@@ -591,6 +616,8 @@
     here = deep_all.at[pl.ds(pl.multiple_of(z * 16, 16), 16)]
     deep_all[pl.ds(pl.multiple_of(z * 16, 16), 16), :] = total
     copies = [send(here, here, zsend.at[6 + d], zrecv.at[6 + d], along(d)) for d in range(1, 8)]
+    strip = send(row_out, row_in, hsend.at[6], hrecv.at[6], beyond)
+    sides += send_sides(1)
     for copy in copies:
         copy.wait()
     all_sum[half * core + own] = deep_all[0:PIECE, :]
@@ -603,13 +630,6 @@
     block = all_sum.at[pl.ds(half * core, half)]
     to_mate = send(block, block, csend.at[1], crecv.at[1], mate)
 
-    for copy in halos:
-        copy.wait()
-    n_row, n_col = lax.axis_size("row"), lax.axis_size("col")
-    row_ok = {-1: r < n_row - 1, 1: r > 0, 0: r >= 0}
-    col_ok = {-1: c < n_col - 1, 1: c > 0, 0: c >= 0}
-    ok = [row_ok[dr] & col_ok[dc] for dr, dc in OFFSETS]
-
     def peak(i, top):
         rows = pl.ds(pl.multiple_of(i * 8, 8), 8)
         power = probe[0, 0, rows, :] ** 2 + probe[0, 1, rows, :] ** 2
@@ -618,33 +638,6 @@
 
     top = lax.fori_loop(0, WIN // 8, peak, jnp.zeros((8, WIN), f32))
     floor = 0.1 * jnp.max(top, axis=(0, 1), keepdims=True)
-
-    for band in range(3):
-
-        def update(i, _, band=band):
-            rows = pl.ds(pl.multiple_of(band * 128 + i * 8, 8), 8)
-            thin = pl.ds(pl.multiple_of(i * 8, 8), 8)
-            for t in range(3):
-                cols = slice(128 * t, 128 * (t + 1))
-                down = weight[rows, cols] + floor
-                for ch in range(2):
-                    g = grad[ch, 1 + t, pl.ds(pl.multiple_of(136 + band * 128 + i * 8, 8), 8), :]
-                    for k, (dr, dc) in enumerate(OFFSETS):
-                        in_rows = dr == 0 or (dr == -1 and band == 2) or (dr == 1 and band == 0)
-                        in_cols = dc == 0 or (dc == -1 and t == 2) or (dc == 1 and t == 0)
-                        if not (in_rows and in_cols):
-                            continue
-                        if k < 2:
-                            v = strips[k, ch, t, thin, :]
-                        elif k < 4:
-                            v = sides[k - 2, ch, 0, rows, :]
-                        else:
-                            v = corners[k - 4, ch, 0, thin, :]
-                        g = g + jnp.where(ok[k], v, 0.0)
-                    obj_new[ch, rows, cols] = obj[ch, rows, cols] + g / down
-            return 0
-
-        lax.fori_loop(0, 16, update, 0)
 
     to_mate.wait()
 
@@ -686,6 +679,32 @@
     mine_count = jnp.sum(jnp.where(is_count, raw[...], 0.0), axis=(0, 1), keepdims=True)
     mean = jnp.sum(sums, axis=0, keepdims=True) / count
     step[...] = jnp.where(rows8.astype(f32) < mine_count, raw[...] - mean, 0.0)
+
+    for copy in sides:
+        copy.wait()
+    strip.wait()
+    for band, start in ((0, outer_to), (1, 128), (2, inner_to)):
+
+        def update(i, _, band=band, start=start):
+            rows = pl.ds(pl.multiple_of(start + i * 8, 8), 8)
+            thin = pl.ds(pl.multiple_of(i * 8, 8), 8)
+            for t in range(3):
+                cols = slice(128 * t, 128 * (t + 1))
+                down = weight[rows, cols] + floor
+                for ch in range(2):
+                    g = grad[ch, 1 + t, pl.ds(pl.multiple_of(136 + start + i * 8, 8), 8), :]
+                    if band == 0:
+                        g = g + jnp.where(outer_ok, row_in[ch, t, thin, :], 0.0)
+                    if band == 2:
+                        g = g + mate_rows[ch, 1 + t, thin, :]
+                    if t == 0:
+                        g = g + jnp.where(col_ok[0], side_in[0, ch, rows, :], 0.0)
+                    if t == 2:
+                        g = g + jnp.where(col_ok[1], side_in[1, ch, rows, :], 0.0)
+                    obj_new[ch, rows, cols] = obj[ch, rows, cols] + g / down
+            return 0
+
+        lax.fori_loop(0, 16, update, 0, unroll=2)
 
 
 def sums(grad, weight, obj, probe, part, raw):
@@ -701,9 +720,12 @@
         in_specs=[v] * 6,
         out_specs=[v] * 3,
         scratch_shapes=[
-            VMEM((2, 2, 3, 128, 128), f32),
-            VMEM((2, 2, 1, TILE, 128), f32),
-            VMEM((4, 2, 1, 128, 128), f32),
+            VMEM((2, 5, 128, 128), f32),
+            VMEM((2, 2, 128, 128), f32),
+            VMEM((2, 3, 128, 128), f32),
+            VMEM((2, 3, 128, 128), f32),
+            VMEM((2, 2, TILE, 128), f32),
+            VMEM((2, 2, TILE, 128), f32),
             VMEM((SHARDS, PIECE, 128), f32),
             VMEM((SHARDS // 2, PIECE, 128), f32),
             VMEM((15, PIECE, 128), f32),
@@ -712,17 +734,17 @@
             VMEM((128, 128), f32),
             VMEM((SHARDS, PIECE, 128), f32),
             VMEM((SHARDS * SHARD, 128), f32),
-            dma((8,)),
-            dma((8,)),
-            dma((2,)),
-            dma((2,)),
+            dma((7,)),
+            dma((7,)),
+            dma((3,)),
+            dma((3,)),
             dma((30,)),
             dma((30,)),
             dma((14,)),
             dma((14,)),
         ],
         compiler_params=pltpu.CompilerParams(
-            collective_id=1, has_side_effects=True, vmem_limit_bytes=50 * 2**20
+            collective_id=1, has_side_effects=True, vmem_limit_bytes=28 * 2**20
         ),
         name="sums",
     )(grad, weight, obj, probe, part, raw)

time: 207 us -> 167 us (0.81)
  Pallas kernels: 194 us -> 159 us
  local copies, waits for them, and re-layouts: 11.1 us -> 7.08 us
    pallas_call x1, Pallas kernels: 55.8 us -> 35.7 us  [slots(): pl.pallas_call(slots_kernel, out_shape=(jax.ShapeDtypeStruct((2, 5, EXT_R...]
    pallas_call x1, Pallas kernels: 78.8 us -> 67.1 us  [sums(): pl.pallas_call(sums_kernel, out_shape=(jax.ShapeDtypeStruct((2, TILE, TIL...]
    unnamed x19 -> x15, local copies, waits for them, and re-layouts: 10.3 us -> 6.34 us
    pallas_call x1, Pallas kernels: 59.3 us -> 55.7 us  [halo(): pl.pallas_call(halo_kernel, out_shape=(jax.ShapeDtypeStruct((2, 5, EXT_RO...]
where the time goes in v2:
time: 167 us
  Pallas kernels  159 us (95%)
  local copies, waits for them, and re-layouts  7.08 us (4%)
    pallas_call x1, Pallas kernels, sums(): pl.pallas_call(sums_kernel, out_shape=(jax.ShapeDtypeStruct((2, TILE, TIL...  67.1 us
    pallas_call x1, Pallas kernels, halo(): pl.pallas_call(halo_kernel, out_shape=(jax.ShapeDtypeStruct((2, 5, EXT_RO...  55.7 us
    pallas_call x1, Pallas kernels, slots(): pl.pallas_call(slots_kernel, out_shape=(jax.ShapeDtypeStruct((2, 5, EXT_R...  35.7 us
    unnamed x15, local copies, waits for them, and re-layouts  6.34 us

profile of v2, /device:TPU:1, one launch (start us, length us, event | category | flops | bytes accessed | tf_op | source)
XLA Modules:
  0.0 167.0 jit_solution(5509057763632899297)
XLA Ops:
  1.3 0.8 copy.12
  2.0 0.1 reshape.15
  2.1 0.1 pad_add_fusion
  2.2 0.0 copy-start
  2.2 1.3 copy-done
  3.5 0.0 copy-start.3
  3.5 1.4 copy-done.3
  4.9 0.0 copy-start.5
  4.9 0.9 copy-done.5
  5.8 0.0 copy-start.2
  5.8 0.0 copy-start.4
  5.8 55.7 %halo_in.1 = (f32[2,5,656,128]{3,2,1,0:T(8,128)S(1)}, f32[6,256,256]{2,1,0:T(8,128)S(1)}, s32[9,8,128]{2,1,0:T(8,128)S(1)}) custom-call(f32[2,384,384]{2,1,0:T(8,128)S(1)} %copy-done, f32[6,256,256]{2,1,0:T(8,128)S(1)} %bitcast.4, s32[8,128]{1,0:T(8,128)S(1)} %pad.4.meta, bf16[256,256]{1,0:T(8,128)(2,1)S(1)} %copy-done.5), custom_call_target="tpu_custom_call" | custom-call | tf_op jit(solution)/shard_map/halo_in/pallas_call | solution.py:164
  61.5 0.0 copy-done.2
  61.5 0.0 copy-done.4
  61.5 0.0 copy-start.1
  61.6 35.7 %slots.1 = (f32[2,5,656,128]{3,2,1,0:T(8,128)S(1)}, f32[384,384]{1,0:T(8,128)S(1)}, f32[5,2,256,128]{3,2,1,0:T(8,128)S(1)}, f32[8,128]{1,0:T(8,128)S(1)}) custom-call(s32[9,8,128]{2,1,0:T(8,128)S(1)} %get-tuple-element.13.where, f32[2,5,656,128]{3,2,1,0:T(8,128)S(1)} %get-tuple-element.14.ext, f32[2,2,256,256]{3,2,1,0:T(8,128)S(1)} %copy-done.2, ...), custom_call_target="tpu_custom_call" | custom-call | tf_op jit(solution)/shard_map/slots/pallas_call | solution.py:432
  97.2 0.0 copy-done.1
  97.2 67.1 %sums.1 = (f32[2,384,384]{2,1,0:T(8,128)S(1)}, f32[2,2,256,256]{3,2,1,0:T(8,128)S(1)}, f32[8,128]{1,0:T(8,128)S(1)}) custom-call(f32[2,5,656,128]{3,2,1,0:T(8,128)S(1)} %get-tuple-element.16.grad, f32[384,384]{1,0:T(8,128)S(1)} %get-tuple-element.17.weight, f32[2,384,384]{2,1,0:T(8,128)S(1)} %copy-done.1, f32[2,2,256,256]{3,2,1,0:T(8,128)S(1)} %copy-done.2, ...), custom_call_target="tpu_custom_call" | custom-call | tf_op jit(solution)/shard_map/sums/pallas_call | solution.py:713
  164.4 0.6 copy.13
  165.0 1.0 copy.17
  166.0 1.0 copy.18
  (1 shorter events, 0.0 us)
Async XLA Ops:
  2.2 1.3 copy-start
  3.5 1.4 copy-start.3
  4.9 0.9 copy-start.5
  5.8 55.7 %copy-start.2 = (f32[2,2,256,256]{3,2,1,0:T(8,128)S(1)}, f32[2,2,256,256]{3,2,1,0:T(8,128)}, u32[]{:S(2)}) copy-start(f32[2,2,256,256]{3,2,1,0:T(8,128)} %probe.3) | copy-start | bytes 3145732
  5.8 55.7 %copy-start.4 = (bf16[8,256,256]{2,1,0:T(8,128)(2,1)S(1)}, bf16[8,256,256]{2,1,0:T(8,128)(2,1)}, u32[]{:S(2)}) copy-start(bf16[8,256,256]{2,1,0:T(8,128)(2,1)} %constant.7.clone.tables) | copy-start | bytes 3145732
  61.5 35.7 %copy-start.1 = (f32[2,384,384]{2,1,0:T(8,128)S(1)}, f32[2,384,384]{2,1,0:T(8,128)}, u32[]{:S(2)}) copy-start(f32[2,384,384]{2,1,0:T(8,128)} %obj.3) | copy-start | bytes 3538948

commit v3 on v2

--- a/solution.py
+++ b/solution.py
@@ -77,8 +77,12 @@
     return copy
 
 
-def halo_kernel(obj, pats, meta, order, ext, spat, metas, turned, ssem, rsem, msend, mrecv):
+def halo_kernel(
+    obj, pats_far, meta, order, ext, spat, metas, pats, turned, lsem, ssem, rsem, msend, mrecv
+):
     core = lax.rem(lax.axis_index("row"), 2)
+    load = pltpu.make_async_copy(pats_far, pats, lsem)
+    load.start()
     greet()
     for t in range(3):
         for ch in range(2):
@@ -91,6 +95,11 @@
     tops = [
         send(strip(1, 3, 136, 128), strip(1, 3, 520, 128), ssem.at[0], rsem.at[0], neighbour((-1, 0))),
         send(strip(1, 3, 392, 128), strip(1, 3, 8, 128), ssem.at[1], rsem.at[1], neighbour((1, 0))),
+    ]
+    left, right = neighbour((0, -1)), neighbour((0, 1))
+    sides = [
+        send(strip(1, 1, 136, 384), strip(4, 1, 136, 384), ssem.at[4], rsem.at[4], left),
+        send(strip(3, 1, 136, 384), strip(0, 1, 136, 384), ssem.at[5], rsem.at[5], right),
     ]
     small = [
         send(
@@ -103,6 +112,8 @@
         for i, (dr, dc) in enumerate(OFFSETS)
     ]
 
+    load.wait()
+
     def reorder(slot, _):
         high, low = split(jnp.sqrt(pats[slot]))
         sorted_cols = mm(high, order[...]) + mm(low, order[...])
@@ -119,14 +130,9 @@
     for copy in tops:
         copy.wait()
     outer = pl.multiple_of(8 + 512 * core, 8)
-    left, right = neighbour((0, -1)), neighbour((0, 1))
     far = [
         send(strip(1, 1, outer, 128), strip(4, 1, outer, 128), ssem.at[2], rsem.at[2], left),
         send(strip(3, 1, outer, 128), strip(0, 1, outer, 128), ssem.at[3], rsem.at[3], right),
-    ]
-    sides = [
-        send(strip(1, 1, 136, 384), strip(4, 1, 136, 384), ssem.at[4], rsem.at[4], left),
-        send(strip(3, 1, 136, 384), strip(0, 1, 136, 384), ssem.at[5], rsem.at[5], right),
     ]
     mate = (lax.axis_index("row") + 1 - 2 * core, lax.axis_index("col"))
     near = pl.multiple_of(392 - 256 * core, 8)
@@ -168,10 +174,17 @@
             jax.ShapeDtypeStruct((CAP, WIN, WIN), f32),
             jax.ShapeDtypeStruct((9, 8, 128), jnp.int32),
         ),
-        in_specs=[pl.BlockSpec(memory_space=VMEM)] * 4,
+        in_specs=[
+            pl.BlockSpec(memory_space=VMEM),
+            pl.BlockSpec(memory_space=pl.ANY),
+            pl.BlockSpec(memory_space=VMEM),
+            pl.BlockSpec(memory_space=VMEM),
+        ],
         out_specs=[pl.BlockSpec(memory_space=VMEM)] * 3,
         scratch_shapes=[
+            VMEM((CAP, WIN, WIN), f32),
             VMEM((2, WIN, 128), f32),
+            pltpu.SemaphoreType.DMA,
             pltpu.SemaphoreType.DMA((8,)),
             pltpu.SemaphoreType.DMA((8,)),
             pltpu.SemaphoreType.DMA((8,)),
@@ -193,7 +206,7 @@
     ext,
     probe,
     spat,
-    tables,
+    tables_far,
     grad,
     weight,
     probe_out,
@@ -206,7 +219,11 @@
     rev,
     power,
     canvas,
+    tables,
+    lsem,
 ):
+    load = pltpu.make_async_copy(tables_far, tables, lsem)
+    load.start()
     r, c = lax.axis_index("row"), lax.axis_index("col")
     row_start, col_start = r * TILE, c * TILE
     lane = lax.broadcasted_iota(jnp.int32, (8, 128), 1)
@@ -276,6 +293,8 @@
 
     for t in range(3):
         weight[:, 128 * t : 128 * (t + 1)] = canvas[2 + t, pl.ds(WIN, TILE), :]
+
+    load.wait()
 
     def visit(slot, _):
         top = where[4, 0, 2 * slot] - row_start + HALF
@@ -335,8 +354,10 @@
                         at = (slice(128 * k, 128 * (k + 1)), slice(128 * ch, 128 * (ch + 1)))
                         ts[m, 2 * q, *at] = high
                         ts[m, 2 * q + 1, *at] = low
-            for q in range(2):
-                zs[m, q] = right_mm(2 + q, ts[m, 2 * q], ts[m, 2 * q + 1])
+        for q in range(2):
+            y = right_mm(2 + q, ts[:, 2 * q].reshape(512, 256), ts[:, 2 * q + 1].reshape(512, 256))
+            for m in range(2):
+                zs[m, q] = y[256 * m : 256 * (m + 1)]
 
         def project(i, _):
             at = pl.ds(pl.multiple_of(i * 16, 16), 16)
@@ -353,9 +374,11 @@
 
         lax.fori_loop(0, 16, project, 0, unroll=True)
 
+        both_a = right_mm(0, ts[:, 0].reshape(512, 256), ts[:, 1].reshape(512, 256))
+        both_b = right_mm(1, ts[:, 2].reshape(512, 256), ts[:, 3].reshape(512, 256))
         for m in range(2):
-            a = right_mm(0, ts[m, 0], ts[m, 1])
-            b = right_mm(1, ts[m, 2], ts[m, 3])
+            a = both_a[256 * m : 256 * (m + 1)]
+            b = both_b[256 * m : 256 * (m + 1)]
             for half, v in enumerate((a + b, a - b)):
                 high, low = split(v)
                 for k in range(2):
@@ -416,7 +439,7 @@
                 grad[ch, tile_g + 2, dst, :] += jnp.where(keep, 0.0, b)
             return tuple(acc)
 
-        acc = lax.fori_loop(0, WIN // STEP, finish, (zero,) * 4, unroll=2)
+        acc = lax.fori_loop(0, WIN // STEP, finish, (zero,) * 4, unroll=True)
         total = [jnp.sum(acc[k], axis=(0, 1), keepdims=True) for k in range(4)]
         at_row = lax.broadcasted_iota(jnp.int32, (8, 128), 0) == slot
         for k in range(2):
@@ -437,7 +460,7 @@
             jax.ShapeDtypeStruct((5, 2, WIN, 128), f32),
             jax.ShapeDtypeStruct((8, 128), f32),
         ),
-        in_specs=[pl.BlockSpec(memory_space=pltpu.SMEM), v, v, v, v],
+        in_specs=[pl.BlockSpec(memory_space=pltpu.SMEM), v, v, v, pl.BlockSpec(memory_space=pl.ANY)],
         out_specs=[v, v, v, v],
         scratch_shapes=[
             VMEM((2, 2, 272, 128), f32),
@@ -448,6 +471,8 @@
             VMEM((2, 2, WIN, WIN), f32),
             VMEM((2, WIN, 128), f32),
             VMEM((8, 904, 128), f32),
+            VMEM((8, WIN, WIN), bf16),
+            pltpu.SemaphoreType.DMA,
         ],
         compiler_params=pltpu.CompilerParams(vmem_limit_bytes=24 * 2**20),
         name="slots",
@@ -553,18 +578,17 @@
     ]
 
     rows_to_mate.wait()
-    for k, tile in enumerate((4, 0)):
-        for ch in range(2):
+    def fill_sides(ch):
+        for k, tile in enumerate((4, 0)):
             side_out[k, ch] = grad[ch, tile, 136:520, :]
             side_out[k, ch, pl.ds(inner_to, 128), :] += mate_rows[ch, tile]
 
-    def send_sides(ch):
-        return [
-            send(side_out.at[k, ch], side_in.at[k, ch], hsend.at[2 + 2 * k + ch], hrecv.at[2 + 2 * k + ch], to)
-            for k, to in enumerate((right, left))
-        ]
-
-    sides = send_sides(0)
+    def send_side(ch, k):
+        i = 2 + 2 * k + ch
+        return send(side_out.at[k, ch], side_in.at[k, ch], hsend.at[i], hrecv.at[i], (right, left)[k])
+
+    fill_sides(0)
+    sides = [send_side(0, 0), send_side(0, 1)]
     to_mate.wait()
 
     def add_mate(i, _):
@@ -579,6 +603,7 @@
         copies.append(
             send(mine.at[half * core + owner], plane_part.at[i], psend.at[i], precv.at[i], to)
         )
+    fill_sides(1)
     for copy in corners:
         copy.wait()
     for ch in range(2):
@@ -608,6 +633,7 @@
                 along(d),
             )
         )
+    sides.append(send_side(1, 0))
     for copy in copies:
         copy.wait()
     total = deep[pl.ds(pl.multiple_of(z * 16, 16), 16), :]
@@ -616,8 +642,8 @@
     here = deep_all.at[pl.ds(pl.multiple_of(z * 16, 16), 16)]
     deep_all[pl.ds(pl.multiple_of(z * 16, 16), 16), :] = total
     copies = [send(here, here, zsend.at[6 + d], zrecv.at[6 + d], along(d)) for d in range(1, 8)]
+    sides.append(send_side(1, 1))
     strip = send(row_out, row_in, hsend.at[6], hrecv.at[6], beyond)
-    sides += send_sides(1)
     for copy in copies:
         copy.wait()
     all_sum[half * core + own] = deep_all[0:PIECE, :]
@@ -682,8 +708,9 @@
 
     for copy in sides:
         copy.wait()
-    strip.wait()
-    for band, start in ((0, outer_to), (1, 128), (2, inner_to)):
+    for band, start in ((1, 128), (2, inner_to), (0, outer_to)):
+        if band == 0:
+            strip.wait()
 
         def update(i, _, band=band, start=start):
             rows = pl.ds(pl.multiple_of(start + i * 8, 8), 8)

time: 167 us -> 157 us (0.940)
  Pallas kernels: 159 us -> 149 us
    pallas_call x1, Pallas kernels: 35.7 us -> 17.2 us  [slots(): pl.pallas_call(slots_kernel, out_shape=(jax.ShapeDtypeStruct((2, 5, EXT_R...]
    pallas_call x1, Pallas kernels: 67.1 us -> 78.1 us  [sums(): pl.pallas_call(sums_kernel, out_shape=(jax.ShapeDtypeStruct((2, TILE, TIL...]
    pallas_call x1, Pallas kernels: 55.7 us -> 53.5 us  [halo(): pl.pallas_call(halo_kernel, out_shape=(jax.ShapeDtypeStruct((2, 5, EXT_RO...]
where the time goes in v3:
time: 157 us
  Pallas kernels  149 us (95%)
  local copies, waits for them, and re-layouts  7.08 us (5%)
    pallas_call x1, Pallas kernels, sums(): pl.pallas_call(sums_kernel, out_shape=(jax.ShapeDtypeStruct((2, TILE, TIL...  78.1 us
    pallas_call x1, Pallas kernels, halo(): pl.pallas_call(halo_kernel, out_shape=(jax.ShapeDtypeStruct((2, 5, EXT_RO...  53.5 us
    pallas_call x1, Pallas kernels, slots(): pl.pallas_call(slots_kernel, out_shape=(jax.ShapeDtypeStruct((2, 5, EXT_R...  17.2 us
    unnamed x15, local copies, waits for them, and re-layouts  6.34 us

profile of v3, /device:TPU:1, one launch (start us, length us, event | category | flops | bytes accessed | tf_op | source)
XLA Modules:
  0.0 157.3 jit_solution(16223405269305160153)
XLA Ops:
  1.3 0.8 copy.12
  2.0 0.1 reshape.15
  2.1 0.1 pad_add_fusion
  2.2 0.0 copy-start
  2.2 1.3 copy-done
  3.5 0.0 copy-start.3
  3.5 1.4 copy-done.3
  4.9 0.0 copy-start.5
  4.9 0.9 copy-done.5
  5.8 0.0 copy-start.2
  5.8 0.0 copy-start.4
  5.8 53.5 %halo_in.1 = (f32[2,5,656,128]{3,2,1,0:T(8,128)S(1)}, f32[6,256,256]{2,1,0:T(8,128)S(1)}, s32[9,8,128]{2,1,0:T(8,128)S(1)}) custom-call(f32[2,384,384]{2,1,0:T(8,128)S(1)} %copy-done, f32[6,256,256]{2,1,0:T(8,128)S(1)} %bitcast.4, s32[8,128]{1,0:T(8,128)S(1)} %pad.4.meta, bf16[256,256]{1,0:T(8,128)(2,1)S(1)} %copy-done.5), custom_call_target="tpu_custom_call" | custom-call | tf_op jit(solution)/shard_map/halo_in/pallas_call | solution.py:170
  59.3 0.0 copy-done.2
  59.3 0.0 copy-done.4
  59.3 0.0 copy-start.1
  59.3 17.2 %slots.1 = (f32[2,5,656,128]{3,2,1,0:T(8,128)S(1)}, f32[384,384]{1,0:T(8,128)S(1)}, f32[5,2,256,128]{3,2,1,0:T(8,128)S(1)}, f32[8,128]{1,0:T(8,128)S(1)}) custom-call(s32[9,8,128]{2,1,0:T(8,128)S(1)} %get-tuple-element.13.where, f32[2,5,656,128]{3,2,1,0:T(8,128)S(1)} %get-tuple-element.14.ext, f32[2,2,256,256]{3,2,1,0:T(8,128)S(1)} %copy-done.2, ...), custom_call_target="tpu_custom_call" | custom-call | tf_op jit(solution)/shard_map/slots/pallas_call | solution.py:455
  76.5 0.0 copy-done.1
  76.5 78.1 %sums.1 = (f32[2,384,384]{2,1,0:T(8,128)S(1)}, f32[2,2,256,256]{3,2,1,0:T(8,128)S(1)}, f32[8,128]{1,0:T(8,128)S(1)}) custom-call(f32[2,5,656,128]{3,2,1,0:T(8,128)S(1)} %get-tuple-element.16.grad, f32[384,384]{1,0:T(8,128)S(1)} %get-tuple-element.17.weight, f32[2,384,384]{2,1,0:T(8,128)S(1)} %copy-done.1, f32[2,2,256,256]{3,2,1,0:T(8,128)S(1)} %copy-done.2, ...), custom_call_target="tpu_custom_call" | custom-call | tf_op jit(solution)/shard_map/sums/pallas_call | solution.py:740
  154.6 0.6 copy.13
  155.3 1.0 copy.17
  156.3 1.0 copy.18
  (1 shorter events, 0.0 us)
Async XLA Ops:
  2.2 1.3 copy-start
  3.5 1.4 copy-start.3
  4.9 0.9 copy-start.5
  5.8 53.5 %copy-start.2 = (f32[2,2,256,256]{3,2,1,0:T(8,128)S(1)}, f32[2,2,256,256]{3,2,1,0:T(8,128)}, u32[]{:S(2)}) copy-start(f32[2,2,256,256]{3,2,1,0:T(8,128)} %probe.3) | copy-start | bytes 3145732
  5.8 53.5 %copy-start.4 = (bf16[8,256,256]{2,1,0:T(8,128)(2,1)S(1)}, bf16[8,256,256]{2,1,0:T(8,128)(2,1)}, u32[]{:S(2)}) copy-start(bf16[8,256,256]{2,1,0:T(8,128)(2,1)} %constant.7.clone.tables_far) | copy-start | bytes 3145732
  59.3 17.2 %copy-start.1 = (f32[2,384,384]{2,1,0:T(8,128)S(1)}, f32[2,384,384]{2,1,0:T(8,128)}, u32[]{:S(2)}) copy-start(f32[2,384,384]{2,1,0:T(8,128)} %obj.3) | copy-start | bytes 3538948

commit v4 on v3

--- a/solution.py
+++ b/solution.py
@@ -176,7 +176,7 @@
         ),
         in_specs=[
             pl.BlockSpec(memory_space=VMEM),
-            pl.BlockSpec(memory_space=pl.ANY),
+            pl.BlockSpec(memory_space=pltpu.HBM),
             pl.BlockSpec(memory_space=VMEM),
             pl.BlockSpec(memory_space=VMEM),
         ],
@@ -261,7 +261,7 @@
 
     lax.fori_loop(0, WIN // 8, fill_power, 0, unroll=4)
 
-    for j in range(9):
+    for j in (0, 1, 2, 3, 5, 6, 7, 8):
         jr, jc = j // 3 - 1, j % 3 - 1
         inside = (r + jr >= 0) & (r + jr < lax.axis_size("row")) & (c + jc >= 0) & (c + jc < lax.axis_size("col"))
         live = jnp.where(inside, where[j, 0, 2 * CAP], 0)
@@ -275,24 +275,29 @@
                 at = left + WIN
                 tile, shift = at // 128, lax.rem(at, 128)
                 keep = lax.broadcasted_iota(jnp.int32, (32, 128), 1) >= shift
-
-                def rows_step(i, _):
-                    src = pl.ds(pl.multiple_of(i * 32, 32), 32)
-                    dst = pl.ds(top + WIN + i * 32, 32)
-                    a, b = turn(power[0, src, :], shift), turn(power[1, src, :], shift)
-                    canvas[tile, dst, :] += jnp.where(keep, a, 0.0)
-                    canvas[tile + 1, dst, :] += jnp.where(keep, b, a)
-                    canvas[tile + 2, dst, :] += jnp.where(keep, 0.0, b)
-                    return 0
-
-                lax.fori_loop(jnp.maximum(-top, 0) // 32, (jnp.minimum(TILE - top, WIN) + 31) // 32, rows_step, 0)
+                begin = jnp.maximum(-top, 0) // 32
+                end = (jnp.minimum(TILE - top, WIN) + 31) // 32
+                for t in range(3):
+
+                    @pl.when((tile + t >= 2) & (tile + t < 5))
+                    def _(t=t):
+                        def rows_step(i, _):
+                            src = pl.ds(pl.multiple_of(i * 32, 32), 32)
+                            a = turn(power[max(t - 1, 0), src, :], shift)
+                            if t == 0:
+                                v = jnp.where(keep, a, 0.0)
+                            elif t == 1:
+                                v = jnp.where(keep, turn(power[1, src, :], shift), a)
+                            else:
+                                v = jnp.where(keep, 0.0, a)
+                            canvas[tile + t, pl.ds(top + WIN + i * 32, 32), :] += v
+                            return 0
+
+                        lax.fori_loop(begin, end, rows_step, 0)
 
             return 0
 
         lax.fori_loop(0, live, place, 0)
-
-    for t in range(3):
-        weight[:, 128 * t : 128 * (t + 1)] = canvas[2 + t, pl.ds(WIN, TILE), :]
 
     load.wait()
 
@@ -300,22 +305,33 @@
         top = where[4, 0, 2 * slot] - row_start + HALF
         left = where[4, 0, 2 * slot + 1] - col_start + HALF
 
-        base = left - 1
-        tile, shift = base // 128, lax.rem(base, 128)
-        last = jnp.minimum(tile + 3, 4)
-        apart = lax.broadcasted_iota(jnp.int32, (512, 256), 0) - lax.broadcasted_iota(
-            jnp.int32, (512, 256), 1
+        tile, shift = left // 128, lax.rem(left, 128)
+        apart = lax.broadcasted_iota(jnp.int32, (256, 128), 0) - lax.broadcasted_iota(
+            jnp.int32, (256, 128), 1
         )
-        move = jnp.where(apart == shift + 1, 1.0, 0.0).astype(bf16)
-        differ = jnp.where(apart == shift + 2, 0.5, jnp.where(apart == shift, -0.5, 0.0)).astype(bf16)
+        move = jnp.where(apart == shift, 1.0, 0.0).astype(bf16)
+        differ = jnp.where(apart == shift + 1, 0.5, jnp.where(apart == shift - 1, -0.5, 0.0)).astype(bf16)
         shifter = jnp.concatenate([move, differ], axis=1)
         for ch in range(2):
-            x = [ext[ch, t, pl.ds(top, 272), :] for t in (tile, tile + 1, tile + 2, last)]
-            high, low = split(jnp.concatenate(x, axis=1))
+            x = [split(ext[ch, tile + t, pl.ds(top, 272), :]) for t in range(3)]
+            high, low = (
+                jnp.concatenate(
+                    [jnp.concatenate([x[j][p], x[j + 1][p]], axis=1) for j in range(2)], axis=0
+                )
+                for p in range(2)
+            )
             y = mm(high, shifter) + mm(low, shifter)
             for j in range(2):
-                patch[ch, j] = y[:, 128 * j : 128 * (j + 1)]
-                slope[ch, j] = y[:, 256 + 128 * j : 256 + 128 * (j + 1)]
+                patch[ch, j] = y[272 * j : 272 * (j + 1), :128]
+                slope[ch, j] = y[272 * j : 272 * (j + 1), 128:]
+
+        @pl.when(shift == 0)
+        def _():
+            first = lax.broadcasted_iota(jnp.int32, (272, 128), 1) == 0
+            for ch in range(2):
+                for j in range(2):
+                    before = turn(ext[ch, tile + j - 1, pl.ds(top, 272), :], 1)
+                    slope[ch, j] += jnp.where(first, -0.5 * before, 0.0)
 
         def leave(i, _):
             rows = [pl.multiple_of(i * 16 + 128 * h, 16) for h in range(2)]
@@ -437,6 +453,11 @@
                 grad[ch, tile_g, dst, :] += jnp.where(keep, a, 0.0)
                 grad[ch, tile_g + 1, dst, :] += jnp.where(keep, b, a)
                 grad[ch, tile_g + 2, dst, :] += jnp.where(keep, 0.0, b)
+            a, b = turn(power[0, at, :], shift_g), turn(power[1, at, :], shift_g)
+            dst = pl.ds(top + HALF + i * STEP, STEP)
+            canvas[tile_g + 1, dst, :] += jnp.where(keep, a, 0.0)
+            canvas[tile_g + 2, dst, :] += jnp.where(keep, b, a)
+            canvas[tile_g + 3, dst, :] += jnp.where(keep, 0.0, b)
             return tuple(acc)
 
         acc = lax.fori_loop(0, WIN // STEP, finish, (zero,) * 4, unroll=True)
@@ -448,6 +469,8 @@
         return 0
 
     lax.fori_loop(0, where[4, 0, 2 * CAP], visit, 0)
+    for t in range(3):
+        weight[:, 128 * t : 128 * (t + 1)] = canvas[2 + t, pl.ds(WIN, TILE), :]
 
 
 def slots(where, ext, probe, spat, tables):
@@ -460,7 +483,7 @@
             jax.ShapeDtypeStruct((5, 2, WIN, 128), f32),
             jax.ShapeDtypeStruct((8, 128), f32),
         ),
-        in_specs=[pl.BlockSpec(memory_space=pltpu.SMEM), v, v, v, pl.BlockSpec(memory_space=pl.ANY)],
+        in_specs=[pl.BlockSpec(memory_space=pltpu.SMEM), v, v, v, pl.BlockSpec(memory_space=pltpu.HBM)],
         out_specs=[v, v, v, v],
         scratch_shapes=[
             VMEM((2, 2, 272, 128), f32),
@@ -564,12 +587,12 @@
     col_ok = [c > 0, c < n_col - 1]
     outer_ok = jnp.where(core == 0, r, n_row - 1 - r) > 0
 
-    rows_to_mate = send(
-        grad.at[:, :, pl.ds(inner_from, 128), :], mate_rows, csend.at[2], crecv.at[2], mate
-    )
     half = SHARDS // 2
     to_mate = send(
         mine.at[pl.ds(half * (1 - core), half)], mate_part, csend.at[0], crecv.at[0], mate
+    )
+    rows_to_mate = send(
+        grad.at[:, :, pl.ds(inner_from, 128), :], mate_rows, csend.at[2], crecv.at[2], mate
     )
     edge = pl.ds(outer_from, 128)
     corners = [

time: 157 us -> 151 us (0.962); the launches traced: 157 us -> 149 us
  Pallas kernels: 149 us -> 141 us
    pallas_call x1, Pallas kernels: 78.1 us -> 66.4 us  [sums(): pl.pallas_call(sums_kernel, out_shape=(jax.ShapeDtypeStruct((2, TILE, TIL...]
    pallas_call x1, Pallas kernels: 17.2 us -> 20.9 us  [slots(): pl.pallas_call(slots_kernel, out_shape=(jax.ShapeDtypeStruct((2, 5, EXT_R...]
where the time goes in v4:
time: 151 us; the launch traced here: 149 us
  Pallas kernels  141 us (93%)
  local copies, waits for them, and re-layouts  7.08 us (5%)
    pallas_call x1, Pallas kernels, sums(): pl.pallas_call(sums_kernel, out_shape=(jax.ShapeDtypeStruct((2, TILE, TIL...  66.4 us
    pallas_call x1, Pallas kernels, halo(): pl.pallas_call(halo_kernel, out_shape=(jax.ShapeDtypeStruct((2, 5, EXT_RO...  53.5 us
    pallas_call x1, Pallas kernels, slots(): pl.pallas_call(slots_kernel, out_shape=(jax.ShapeDtypeStruct((2, 5, EXT_R...  20.9 us
    unnamed x15, local copies, waits for them, and re-layouts  6.34 us

profile of v4, /device:TPU:1, one launch (start us, length us, event | category | flops | bytes accessed | tf_op | source)
XLA Modules:
  0.0 149.3 jit_solution(879654318833512812)
XLA Ops:
  1.3 0.8 copy.12
  2.0 0.1 reshape.15
  2.1 0.1 pad_add_fusion
  2.2 0.0 copy-start
  2.2 1.3 copy-done
  3.5 0.0 copy-start.3
  3.5 1.4 copy-done.3
  4.9 0.0 copy-start.5
  4.9 0.9 copy-done.5
  5.8 0.0 copy-start.2
  5.8 0.0 copy-start.4
  5.8 53.5 %halo_in.1 = (f32[2,5,656,128]{3,2,1,0:T(8,128)S(1)}, f32[6,256,256]{2,1,0:T(8,128)S(1)}, s32[9,8,128]{2,1,0:T(8,128)S(1)}) custom-call(f32[2,384,384]{2,1,0:T(8,128)S(1)} %copy-done, f32[6,256,256]{2,1,0:T(8,128)S(1)} %bitcast.4, s32[8,128]{1,0:T(8,128)S(1)} %pad.4.meta, bf16[256,256]{1,0:T(8,128)(2,1)S(1)} %copy-done.5), custom_call_target="tpu_custom_call" | custom-call | tf_op jit(solution)/shard_map/halo_in/pallas_call | solution.py:170
  59.3 0.0 copy-done.2
  59.3 0.0 copy-done.4
  59.3 0.0 copy-start.1
  59.3 20.9 %slots.1 = (f32[2,5,656,128]{3,2,1,0:T(8,128)S(1)}, f32[384,384]{1,0:T(8,128)S(1)}, f32[5,2,256,128]{3,2,1,0:T(8,128)S(1)}, f32[8,128]{1,0:T(8,128)S(1)}) custom-call(s32[9,8,128]{2,1,0:T(8,128)S(1)} %get-tuple-element.13.where, f32[2,5,656,128]{3,2,1,0:T(8,128)S(1)} %get-tuple-element.14.ext, f32[2,2,256,256]{3,2,1,0:T(8,128)S(1)} %copy-done.2, ...), custom_call_target="tpu_custom_call" | custom-call | tf_op jit(solution)/shard_map/slots/pallas_call | solution.py:478
  80.2 0.0 copy-done.1
  80.2 66.4 %sums.1 = (f32[2,384,384]{2,1,0:T(8,128)S(1)}, f32[2,2,256,256]{3,2,1,0:T(8,128)S(1)}, f32[8,128]{1,0:T(8,128)S(1)}) custom-call(f32[2,5,656,128]{3,2,1,0:T(8,128)S(1)} %get-tuple-element.16.grad, f32[384,384]{1,0:T(8,128)S(1)} %get-tuple-element.17.weight, f32[2,384,384]{2,1,0:T(8,128)S(1)} %copy-done.1, f32[2,2,256,256]{3,2,1,0:T(8,128)S(1)} %copy-done.2, ...), custom_call_target="tpu_custom_call" | custom-call | tf_op jit(solution)/shard_map/sums/pallas_call | solution.py:763
  146.6 0.6 copy.13
  147.3 1.0 copy.17
  148.3 1.0 copy.18
  (1 shorter events, 0.0 us)
Async XLA Ops:
  2.2 1.3 copy-start
  3.5 1.4 copy-start.3
  4.9 0.9 copy-start.5
  5.8 53.5 %copy-start.2 = (f32[2,2,256,256]{3,2,1,0:T(8,128)S(1)}, f32[2,2,256,256]{3,2,1,0:T(8,128)}, u32[]{:S(2)}) copy-start(f32[2,2,256,256]{3,2,1,0:T(8,128)} %probe.3) | copy-start | bytes 3145732
  5.8 53.5 %copy-start.4 = (bf16[8,256,256]{2,1,0:T(8,128)(2,1)S(1)}, bf16[8,256,256]{2,1,0:T(8,128)(2,1)}, u32[]{:S(2)}) copy-start(bf16[8,256,256]{2,1,0:T(8,128)(2,1)} %constant.7.clone.tables_far) | copy-start | bytes 3145732
  59.3 21.0 %copy-start.1 = (f32[2,384,384]{2,1,0:T(8,128)S(1)}, f32[2,384,384]{2,1,0:T(8,128)}, u32[]{:S(2)}) copy-start(f32[2,384,384]{2,1,0:T(8,128)} %obj.3) | copy-start | bytes 3538948

commit v5 on v4

--- a/solution.py
+++ b/solution.py
@@ -39,14 +39,6 @@
     return np.stack(out)
 
 
-def order_table():
-    table = np.zeros((WIN, WIN), np.float32)
-    k = np.arange(HALF)
-    table[2 * k, k] = 1
-    table[2 * k + 1, HALF + k] = 1
-    return table.astype(ml_dtypes.bfloat16)
-
-
 def split(x):
     high = x.astype(bf16)
     return high, (x - high.astype(f32)).astype(bf16)
@@ -77,12 +69,45 @@
     return copy
 
 
+def when(condition, act):
+    @pl.when(condition)
+    def _():
+        act()
+
+
+def finish_copy(copy, sent, received):
+    when(sent, copy.wait_send)
+    when(received, copy.wait_recv)
+
+
+def make(src, dst, ssem, rsem, to):
+    return pltpu.make_async_remote_copy(
+        src_ref=src, dst_ref=dst, send_sem=ssem, recv_sem=rsem, device_id=to, device_id_type=MESH
+    )
+
+
 def halo_kernel(
-    obj, pats_far, meta, order, ext, spat, metas, pats, turned, lsem, ssem, rsem, msend, mrecv
+    obj, pats_far, meta, ext, spat, metas, pats, turned, lsem, ssem, rsem, msend, mrecv
 ):
-    core = lax.rem(lax.axis_index("row"), 2)
+    r, c = lax.axis_index("row"), lax.axis_index("col")
+    core = lax.rem(r, 2)
     load = pltpu.make_async_copy(pats_far, pats, lsem)
     load.start()
+    has_up, has_down = r > 0, r < lax.axis_size("row") - 1
+    has_left, has_right = c > 0, c < lax.axis_size("col") - 1
+
+    for ch in range(2):
+        for t in range(5):
+            ext[ch, t, 0:8, :] = jnp.zeros((8, 128), f32)
+            ext[ch, t, 648:656, :] = jnp.zeros((8, 128), f32)
+
+    def blank(tiles, rows):
+        ext[:, tiles, rows, :] = jnp.zeros((2, tiles.stop - tiles.start, rows.stop - rows.start, 128), f32)
+
+    when(r == 0, lambda: blank(slice(0, 5), slice(8, 136)))
+    when(jnp.logical_not(has_down), lambda: blank(slice(0, 5), slice(520, 648)))
+    when(c == 0, lambda: blank(slice(0, 1), slice(8, 648)))
+    when(jnp.logical_not(has_right), lambda: blank(slice(4, 5), slice(8, 648)))
     greet()
     for t in range(3):
         for ch in range(2):
@@ -92,15 +117,17 @@
     def strip(tile, tiles, row, rows):
         return ext.at[:, pl.ds(tile, tiles), pl.ds(row, rows), :]
 
-    tops = [
-        send(strip(1, 3, 136, 128), strip(1, 3, 520, 128), ssem.at[0], rsem.at[0], neighbour((-1, 0))),
-        send(strip(1, 3, 392, 128), strip(1, 3, 8, 128), ssem.at[1], rsem.at[1], neighbour((1, 0))),
-    ]
     left, right = neighbour((0, -1)), neighbour((0, 1))
-    sides = [
-        send(strip(1, 1, 136, 384), strip(4, 1, 136, 384), ssem.at[4], rsem.at[4], left),
-        send(strip(3, 1, 136, 384), strip(0, 1, 136, 384), ssem.at[5], rsem.at[5], right),
-    ]
+    outer = pl.multiple_of(8 + 512 * core, 8)
+    up = make(strip(1, 3, 136, 128), strip(1, 3, 520, 128), ssem.at[0], rsem.at[0], neighbour((-1, 0)))
+    down = make(strip(1, 3, 392, 128), strip(1, 3, 8, 128), ssem.at[1], rsem.at[1], neighbour((1, 0)))
+    to_left = make(strip(1, 1, 136, 384), strip(4, 1, 136, 384), ssem.at[4], rsem.at[4], left)
+    to_right = make(strip(3, 1, 136, 384), strip(0, 1, 136, 384), ssem.at[5], rsem.at[5], right)
+    when(has_up, up.start)
+    when(has_down, down.start)
+    far_left, far_right = lax.rem(c, 4) == 0, lax.rem(c, 4) == 3
+    when(has_left & far_left, to_left.start)
+    when(has_right & far_right, to_right.start)
     small = [
         send(
             metas.at[4],
@@ -111,12 +138,19 @@
         )
         for i, (dr, dc) in enumerate(OFFSETS)
     ]
-
+    when(has_left & jnp.logical_not(far_left), to_left.start)
+    when(has_right & jnp.logical_not(far_right), to_right.start)
     load.wait()
+    order = []
+    for parity in range(2):
+        index = lax.broadcasted_iota(jnp.int32, (WIN, HALF), 0)
+        wanted = 2 * lax.broadcasted_iota(jnp.int32, (WIN, HALF), 1) + parity
+        order.append(jnp.where(index == wanted, 1.0, 0.0).astype(bf16))
+    order = jnp.concatenate(order, axis=1)
 
     def reorder(slot, _):
         high, low = split(jnp.sqrt(pats[slot]))
-        sorted_cols = mm(high, order[...]) + mm(low, order[...])
+        sorted_cols = mm(high, order) + mm(low, order)
         for j in range(2):
             turned[j] = sorted_cols[:, 128 * j : 128 * (j + 1)]
         for parity in range(2):
@@ -127,46 +161,29 @@
         return 0
 
     lax.fori_loop(0, CAP, reorder, 0)
-    for copy in tops:
-        copy.wait()
-    outer = pl.multiple_of(8 + 512 * core, 8)
-    far = [
-        send(strip(1, 1, outer, 128), strip(4, 1, outer, 128), ssem.at[2], rsem.at[2], left),
-        send(strip(3, 1, outer, 128), strip(0, 1, outer, 128), ssem.at[3], rsem.at[3], right),
-    ]
-    mate = (lax.axis_index("row") + 1 - 2 * core, lax.axis_index("col"))
+    finish_copy(up, has_up, has_down)
+    finish_copy(down, has_down, has_up)
+    far_l = make(strip(1, 1, outer, 128), strip(4, 1, outer, 128), ssem.at[2], rsem.at[2], left)
+    far_r = make(strip(3, 1, outer, 128), strip(0, 1, outer, 128), ssem.at[3], rsem.at[3], right)
+    when(has_left, far_l.start)
+    when(has_right, far_r.start)
+    mate = (r + 1 - 2 * core, c)
     near = pl.multiple_of(392 - 256 * core, 8)
-    for k, tile in enumerate((4, 0)):
-        sides[k].wait()
-        far.append(
+    relays = []
+    for k, (tile, copy, sent, received) in enumerate(
+        ((4, to_left, has_left, has_right), (0, to_right, has_right, has_left))
+    ):
+        finish_copy(copy, sent, received)
+        relays.append(
             send(strip(tile, 1, near, 128), strip(tile, 1, outer, 128), ssem.at[6 + k], rsem.at[6 + k], mate)
         )
-    for copy in far + small:
+    finish_copy(far_l, has_left, has_right)
+    finish_copy(far_r, has_right, has_left)
+    for copy in relays + small:
         copy.wait()
-    r, c = lax.axis_index("row"), lax.axis_index("col")
-    for ch in range(2):
-        for t in range(5):
-            ext[ch, t, 0:8, :] = jnp.zeros((8, 128), f32)
-            ext[ch, t, 648:656, :] = jnp.zeros((8, 128), f32)
-
-    @pl.when(r == 0)
-    def _():
-        ext[:, :, 8:136, :] = jnp.zeros((2, 5, 128, 128), f32)
-
-    @pl.when(r == lax.axis_size("row") - 1)
-    def _():
-        ext[:, :, 520:648, :] = jnp.zeros((2, 5, 128, 128), f32)
-
-    @pl.when(c == 0)
-    def _():
-        ext[:, 0, 8:648, :] = jnp.zeros((2, 640, 128), f32)
-
-    @pl.when(c == lax.axis_size("col") - 1)
-    def _():
-        ext[:, 4, 8:648, :] = jnp.zeros((2, 640, 128), f32)
-
-
-def halo(obj, pats, meta, order):
+
+
+def halo(obj, pats, meta):
     return pl.pallas_call(
         halo_kernel,
         out_shape=(
@@ -177,7 +194,6 @@
         in_specs=[
             pl.BlockSpec(memory_space=VMEM),
             pl.BlockSpec(memory_space=pltpu.HBM),
-            pl.BlockSpec(memory_space=VMEM),
             pl.BlockSpec(memory_space=VMEM),
         ],
         out_specs=[pl.BlockSpec(memory_space=VMEM)] * 3,
@@ -194,7 +210,7 @@
             collective_id=0, has_side_effects=True, vmem_limit_bytes=20 * 2**20
         ),
         name="halo_in",
-    )(obj, pats, meta, order)
+    )(obj, pats, meta)
 
 
 def turn(x, shift):
@@ -266,7 +282,7 @@
         inside = (r + jr >= 0) & (r + jr < lax.axis_size("row")) & (c + jc >= 0) & (c + jc < lax.axis_size("col"))
         live = jnp.where(inside, where[j, 0, 2 * CAP], 0)
 
-        def place(slot, _, j=j):
+        def place(slot, _, j=j, jr=jr, jc=jc):
             top = where[j, 0, 2 * slot] - row_start
             left = where[j, 0, 2 * slot + 1] - col_start
 
@@ -274,26 +290,18 @@
             def _():
                 at = left + WIN
                 tile, shift = at // 128, lax.rem(at, 128)
-                keep = lax.broadcasted_iota(jnp.int32, (32, 128), 1) >= shift
-                begin = jnp.maximum(-top, 0) // 32
-                end = (jnp.minimum(TILE - top, WIN) + 31) // 32
-                for t in range(3):
-
-                    @pl.when((tile + t >= 2) & (tile + t < 5))
-                    def _(t=t):
-                        def rows_step(i, _):
-                            src = pl.ds(pl.multiple_of(i * 32, 32), 32)
-                            a = turn(power[max(t - 1, 0), src, :], shift)
-                            if t == 0:
-                                v = jnp.where(keep, a, 0.0)
-                            elif t == 1:
-                                v = jnp.where(keep, turn(power[1, src, :], shift), a)
-                            else:
-                                v = jnp.where(keep, 0.0, a)
-                            canvas[tile + t, pl.ds(top + WIN + i * 32, 32), :] += v
-                            return 0
-
-                        lax.fori_loop(begin, end, rows_step, 0)
+                begin, rows = {-1: (HALF, HALF), 0: (0, WIN), 1: (0, HALF)}[jr]
+                for start in range(begin, begin + rows, 64):
+                    keep = lax.broadcasted_iota(jnp.int32, (64, 128), 1) >= shift
+                    dst = pl.ds(top + WIN + start, 64)
+                    if jc <= 0:
+                        b = turn(power[1, start : start + 64, :], shift)
+                        canvas[tile + 2, dst, :] += jnp.where(keep, 0.0, b)
+                    if jc >= 0:
+                        a = turn(power[0, start : start + 64, :], shift)
+                        canvas[tile, dst, :] += jnp.where(keep, a, 0.0)
+                    if jc == 0:
+                        canvas[tile + 1, dst, :] += jnp.where(keep, b, a)
 
             return 0
 
@@ -595,10 +603,11 @@
         grad.at[:, :, pl.ds(inner_from, 128), :], mate_rows, csend.at[2], crecv.at[2], mate
     )
     edge = pl.ds(outer_from, 128)
-    corners = [
-        send(grad.at[:, 4, edge, :], corner_in.at[0], hsend.at[0], hrecv.at[0], right),
-        send(grad.at[:, 0, edge, :], corner_in.at[1], hsend.at[1], hrecv.at[1], left),
-    ]
+    has_left, has_right = col_ok
+    corner_r = make(grad.at[:, 4, edge, :], corner_in.at[0], hsend.at[0], hrecv.at[0], right)
+    corner_l = make(grad.at[:, 0, edge, :], corner_in.at[1], hsend.at[1], hrecv.at[1], left)
+    when(has_right, corner_r.start)
+    when(has_left, corner_l.start)
 
     rows_to_mate.wait()
     def fill_sides(ch):
@@ -606,12 +615,14 @@
             side_out[k, ch] = grad[ch, tile, 136:520, :]
             side_out[k, ch, pl.ds(inner_to, 128), :] += mate_rows[ch, tile]
 
-    def send_side(ch, k):
+    def side(ch, k):
         i = 2 + 2 * k + ch
-        return send(side_out.at[k, ch], side_in.at[k, ch], hsend.at[i], hrecv.at[i], (right, left)[k])
+        return make(side_out.at[k, ch], side_in.at[k, ch], hsend.at[i], hrecv.at[i], (right, left)[k])
+
+    sides = [[side(ch, k) for k in range(2)] for ch in range(2)]
 
     fill_sides(0)
-    sides = [send_side(0, 0), send_side(0, 1)]
+    fill_sides(1)
     to_mate.wait()
 
     def add_mate(i, _):
@@ -626,9 +637,8 @@
         copies.append(
             send(mine.at[half * core + owner], plane_part.at[i], psend.at[i], precv.at[i], to)
         )
-    fill_sides(1)
-    for copy in corners:
-        copy.wait()
+    finish_copy(corner_r, has_right, has_left)
+    finish_copy(corner_l, has_left, has_right)
     for ch in range(2):
         for t in range(3):
             v = grad[ch, 1 + t, edge, :]
@@ -637,6 +647,8 @@
             if t == 2:
                 v = v + jnp.where(col_ok[1], corner_in[1, ch], 0.0)
             row_out[ch, t] = v
+    strip = make(row_out, row_in, hsend.at[6], hrecv.at[6], beyond)
+    when(outer_ok, strip.start)
     for copy in copies:
         copy.wait()
     total = mine[half * core + own]
@@ -656,7 +668,6 @@
                 along(d),
             )
         )
-    sides.append(send_side(1, 0))
     for copy in copies:
         copy.wait()
     total = deep[pl.ds(pl.multiple_of(z * 16, 16), 16), :]
@@ -665,8 +676,9 @@
     here = deep_all.at[pl.ds(pl.multiple_of(z * 16, 16), 16)]
     deep_all[pl.ds(pl.multiple_of(z * 16, 16), 16), :] = total
     copies = [send(here, here, zsend.at[6 + d], zrecv.at[6 + d], along(d)) for d in range(1, 8)]
-    sides.append(send_side(1, 1))
-    strip = send(row_out, row_in, hsend.at[6], hrecv.at[6], beyond)
+    for ch in range(2):
+        when(has_right, sides[ch][0].start)
+        when(has_left, sides[ch][1].start)
     for copy in copies:
         copy.wait()
     all_sum[half * core + own] = deep_all[0:PIECE, :]
@@ -729,11 +741,12 @@
     mean = jnp.sum(sums, axis=0, keepdims=True) / count
     step[...] = jnp.where(rows8.astype(f32) < mine_count, raw[...] - mean, 0.0)
 
-    for copy in sides:
-        copy.wait()
+    for ch in range(2):
+        finish_copy(sides[ch][0], has_right, has_left)
+        finish_copy(sides[ch][1], has_left, has_right)
     for band, start in ((1, 128), (2, inner_to), (0, outer_to)):
         if band == 0:
-            strip.wait()
+            finish_copy(strip, outer_ok, outer_ok)
 
         def update(i, _, band=band, start=start):
             rows = pl.ds(pl.multiple_of(start + i * 8, 8), 8)
@@ -803,7 +816,7 @@
 def on_device(object_field, probe, patterns, positions, counts):
     meta = jnp.concatenate([positions.reshape(1, 2 * CAP), counts.reshape(1, 1)], axis=1)
     meta = jnp.pad(meta, ((0, 7), (0, 128 - 2 * CAP - 1)))
-    ext, spat, where = halo(object_field, patterns[0, 0], meta, jnp.asarray(order_table()))
+    ext, spat, where = halo(object_field, patterns[0, 0], meta)
     grad, weight, part, raw = slots(where, ext, probe, spat, jnp.asarray(dft_tables()))
     object_new, probe_new, step = sums(
         grad, weight, object_field, probe, part.reshape(SHARDS * SHARD, 128), raw

time: 151 us -> 142 us (0.940); the launches traced: 149 us -> 142 us
  Pallas kernels: 141 us -> 134 us
    pallas_call x1, Pallas kernels: 53.5 us -> 39.8 us  [halo(): pl.pallas_call(halo_kernel, out_shape=(jax.ShapeDtypeStruct((2, 5, EXT_RO...]
    pallas_call x1, Pallas kernels: 66.4 us -> 79.4 us  [sums(): pl.pallas_call(sums_kernel, out_shape=(jax.ShapeDtypeStruct((2, TILE, TIL...]
    pallas_call x1, Pallas kernels: 20.9 us -> 15 us  [slots(): pl.pallas_call(slots_kernel, out_shape=(jax.ShapeDtypeStruct((2, 5, EXT_R...]
    unnamed x15 -> x13, local copies, waits for them, and re-layouts: 6.34 us -> 5.44 us
where the time goes in v5:
time: 142 us
  Pallas kernels  134 us (94%)
  local copies, waits for them, and re-layouts  6.18 us (4%)
    pallas_call x1, Pallas kernels, sums(): pl.pallas_call(sums_kernel, out_shape=(jax.ShapeDtypeStruct((2, TILE, TIL...  79.4 us
    pallas_call x1, Pallas kernels, halo(): pl.pallas_call(halo_kernel, out_shape=(jax.ShapeDtypeStruct((2, 5, EXT_RO...  39.8 us
    pallas_call x1, Pallas kernels, slots(): pl.pallas_call(slots_kernel, out_shape=(jax.ShapeDtypeStruct((2, 5, EXT_R...  15 us
    unnamed x13, local copies, waits for them, and re-layouts  5.44 us

profile of v5, /device:TPU:1, one launch (start us, length us, event | category | flops | bytes accessed | tf_op | source)
XLA Modules:
  0.0 141.9 jit_solution(7911714059592295971)
XLA Ops:
  1.3 0.8 copy.11
  2.0 0.1 reshape.15
  2.1 0.1 pad_add_fusion
  2.2 0.0 copy-start
  2.2 1.3 copy-done
  3.5 0.0 copy-start.3
  3.5 1.4 copy-done.3
  4.9 0.0 copy-start.2
  4.9 0.0 copy-start.4
  4.9 39.8 %halo_in.1 = (f32[2,5,656,128]{3,2,1,0:T(8,128)S(1)}, f32[6,256,256]{2,1,0:T(8,128)S(1)}, s32[9,8,128]{2,1,0:T(8,128)S(1)}) custom-call(f32[2,384,384]{2,1,0:T(8,128)S(1)} %copy-done, f32[6,256,256]{2,1,0:T(8,128)S(1)} %bitcast.4, s32[8,128]{1,0:T(8,128)S(1)} %pad.4.meta), custom_call_target="tpu_custom_call" | custom-call | tf_op jit(solution)/shard_map/halo_in/pallas_call | solution.py:187
  44.8 0.0 copy-done.2
  44.8 0.0 copy-done.4
  44.8 0.0 copy-start.1
  44.8 15.0 %slots.1 = (f32[2,5,656,128]{3,2,1,0:T(8,128)S(1)}, f32[384,384]{1,0:T(8,128)S(1)}, f32[5,2,256,128]{3,2,1,0:T(8,128)S(1)}, f32[8,128]{1,0:T(8,128)S(1)}) custom-call(s32[9,8,128]{2,1,0:T(8,128)S(1)} %get-tuple-element.13.where, f32[2,5,656,128]{3,2,1,0:T(8,128)S(1)} %get-tuple-element.14.ext, f32[2,2,256,256]{3,2,1,0:T(8,128)S(1)} %copy-done.2, ...), custom_call_target="tpu_custom_call" | custom-call | tf_op jit(solution)/shard_map/slots/pallas_call | solution.py:486
  59.8 0.0 copy-done.1
  59.8 79.4 %sums.1 = (f32[2,384,384]{2,1,0:T(8,128)S(1)}, f32[2,2,256,256]{3,2,1,0:T(8,128)S(1)}, f32[8,128]{1,0:T(8,128)S(1)}) custom-call(f32[2,5,656,128]{3,2,1,0:T(8,128)S(1)} %get-tuple-element.16.grad, f32[384,384]{1,0:T(8,128)S(1)} %get-tuple-element.17.weight, f32[2,384,384]{2,1,0:T(8,128)S(1)} %copy-done.1, f32[2,2,256,256]{3,2,1,0:T(8,128)S(1)} %copy-done.2, ...), custom_call_target="tpu_custom_call" | custom-call | tf_op jit(solution)/shard_map/sums/pallas_call | solution.py:776
  139.3 0.6 copy.12
  139.9 1.0 copy.16
  140.9 1.0 copy.17
  (1 shorter events, 0.0 us)
Async XLA Ops:
  2.2 1.3 copy-start
  3.5 1.4 copy-start.3
  4.9 39.9 %copy-start.2 = (f32[2,2,256,256]{3,2,1,0:T(8,128)S(1)}, f32[2,2,256,256]{3,2,1,0:T(8,128)}, u32[]{:S(2)}) copy-start(f32[2,2,256,256]{3,2,1,0:T(8,128)} %probe.3) | copy-start | bytes 3145732
  4.9 39.9 %copy-start.4 = (bf16[8,256,256]{2,1,0:T(8,128)(2,1)S(1)}, bf16[8,256,256]{2,1,0:T(8,128)(2,1)}, u32[]{:S(2)}) copy-start(bf16[8,256,256]{2,1,0:T(8,128)(2,1)} %constant.4.clone.tables_far) | copy-start | bytes 3145732
  44.8 15.1 %copy-start.1 = (f32[2,384,384]{2,1,0:T(8,128)S(1)}, f32[2,384,384]{2,1,0:T(8,128)}, u32[]{:S(2)}) copy-start(f32[2,384,384]{2,1,0:T(8,128)} %obj.3) | copy-start | bytes 3538948

commit v6 on v5

--- a/solution.py
+++ b/solution.py
@@ -128,6 +128,17 @@
     far_left, far_right = lax.rem(c, 4) == 0, lax.rem(c, 4) == 3
     when(has_left & far_left, to_left.start)
     when(has_right & far_right, to_right.start)
+    beyond = lax.rem(r - 1 + 2 * core + lax.axis_size("row"), lax.axis_size("row"))
+    outer_ok = jnp.where(core == 0, r, lax.axis_size("row") - 1 - r) > 0
+    own_edge, its_edge = pl.multiple_of(136 + 256 * core, 8), pl.multiple_of(520 - 512 * core, 8)
+    jump_l = make(
+        strip(1, 1, own_edge, 128), strip(4, 1, its_edge, 128), ssem.at[2], rsem.at[2], (beyond, left[1])
+    )
+    jump_r = make(
+        strip(3, 1, own_edge, 128), strip(0, 1, its_edge, 128), ssem.at[3], rsem.at[3], (beyond, right[1])
+    )
+    when(has_left & far_left & outer_ok, jump_l.start)
+    when(has_right & far_right & outer_ok, jump_r.start)
     small = [
         send(
             metas.at[4],
@@ -165,8 +176,8 @@
     finish_copy(down, has_down, has_up)
     far_l = make(strip(1, 1, outer, 128), strip(4, 1, outer, 128), ssem.at[2], rsem.at[2], left)
     far_r = make(strip(3, 1, outer, 128), strip(0, 1, outer, 128), ssem.at[3], rsem.at[3], right)
-    when(has_left, far_l.start)
-    when(has_right, far_r.start)
+    when(has_left & jnp.logical_not(far_left), far_l.start)
+    when(has_right & jnp.logical_not(far_right), far_r.start)
     mate = (r + 1 - 2 * core, c)
     near = pl.multiple_of(392 - 256 * core, 8)
     relays = []
@@ -177,8 +188,10 @@
         relays.append(
             send(strip(tile, 1, near, 128), strip(tile, 1, outer, 128), ssem.at[6 + k], rsem.at[6 + k], mate)
         )
-    finish_copy(far_l, has_left, has_right)
-    finish_copy(far_r, has_right, has_left)
+    sent_left = has_left & (jnp.logical_not(far_left) | outer_ok)
+    sent_right = has_right & (jnp.logical_not(far_right) | outer_ok)
+    finish_copy(far_l, sent_left, sent_right)
+    finish_copy(far_r, sent_right, sent_left)
     for copy in relays + small:
         copy.wait()
 
@@ -575,7 +588,7 @@
     planes = [(dx, dy) for dx in range(4) for dy in range(4) if (dx, dy) != (0, 0)]
 
     barrier = pltpu.get_barrier_semaphore()
-    partners = [left, right, mate, beyond]
+    partners = [left, right, mate, beyond, (beyond[0], left[1]), (beyond[0], right[1])]
     partners += [plane(*p) for p in planes] + [along(d) for d in range(1, 8)]
     for partner in partners:
         pl.semaphore_signal(barrier, inc=1, device_id=partner, device_id_type=MESH)
@@ -604,10 +617,20 @@
     )
     edge = pl.ds(outer_from, 128)
     has_left, has_right = col_ok
-    corner_r = make(grad.at[:, 4, edge, :], corner_in.at[0], hsend.at[0], hrecv.at[0], right)
-    corner_l = make(grad.at[:, 0, edge, :], corner_in.at[1], hsend.at[1], hrecv.at[1], left)
-    when(has_right, corner_r.start)
-    when(has_left, corner_l.start)
+    far_left, far_right = lax.rem(c, 4) == 0, lax.rem(c, 4) == 3
+
+    def corner(tile, k, to):
+        return make(grad.at[:, tile, edge, :], corner_in.at[k], hsend.at[k], hrecv.at[k], to)
+
+    corner_r, corner_l = corner(4, 0, right), corner(0, 1, left)
+    jump_r, jump_l = corner(4, 0, (beyond[0], right[1])), corner(0, 1, (beyond[0], left[1]))
+    when(has_right & jnp.logical_not(far_right), corner_r.start)
+    when(has_left & jnp.logical_not(far_left), corner_l.start)
+    when(has_right & far_right & outer_ok, jump_r.start)
+    when(has_left & far_left & outer_ok, jump_l.start)
+    corner_left = has_left & (jnp.logical_not(far_left) | outer_ok)
+    corner_right = has_right & (jnp.logical_not(far_right) | outer_ok)
+    jumped = [has_left & far_left & outer_ok, has_right & far_right & outer_ok]
 
     rows_to_mate.wait()
     def fill_sides(ch):
@@ -637,15 +660,15 @@
         copies.append(
             send(mine.at[half * core + owner], plane_part.at[i], psend.at[i], precv.at[i], to)
         )
-    finish_copy(corner_r, has_right, has_left)
-    finish_copy(corner_l, has_left, has_right)
+    finish_copy(corner_r, corner_right, corner_left)
+    finish_copy(corner_l, corner_left, corner_right)
     for ch in range(2):
         for t in range(3):
             v = grad[ch, 1 + t, edge, :]
             if t == 0:
-                v = v + jnp.where(col_ok[0], corner_in[0, ch], 0.0)
+                v = v + jnp.where(has_left & jnp.logical_not(far_left), corner_in[0, ch], 0.0)
             if t == 2:
-                v = v + jnp.where(col_ok[1], corner_in[1, ch], 0.0)
+                v = v + jnp.where(has_right & jnp.logical_not(far_right), corner_in[1, ch], 0.0)
             row_out[ch, t] = v
     strip = make(row_out, row_in, hsend.at[6], hrecv.at[6], beyond)
     when(outer_ok, strip.start)
@@ -758,6 +781,8 @@
                     g = grad[ch, 1 + t, pl.ds(pl.multiple_of(136 + start + i * 8, 8), 8), :]
                     if band == 0:
                         g = g + jnp.where(outer_ok, row_in[ch, t, thin, :], 0.0)
+                        if t != 1:
+                            g = g + jnp.where(jumped[t // 2], corner_in[t // 2, ch, thin, :], 0.0)
                     if band == 2:
                         g = g + mate_rows[ch, 1 + t, thin, :]
                     if t == 0:

time: 142 us -> 142 us (level)
    pallas_call x1, Pallas kernels: 15 us -> 6.52 us  [slots(): pl.pallas_call(slots_kernel, out_shape=(jax.ShapeDtypeStruct((2, 5, EXT_R...]
    pallas_call x1, Pallas kernels: 79.4 us -> 87.4 us  [sums(): pl.pallas_call(sums_kernel, out_shape=(jax.ShapeDtypeStruct((2, TILE, TIL...]
where the time goes in v6:
time: 142 us; the launch traced here: 141 us
  Pallas kernels  134 us (94%)
  local copies, waits for them, and re-layouts  6.18 us (4%)
    pallas_call x1, Pallas kernels, sums(): pl.pallas_call(sums_kernel, out_shape=(jax.ShapeDtypeStruct((2, TILE, TIL...  87.4 us
    pallas_call x1, Pallas kernels, halo(): pl.pallas_call(halo_kernel, out_shape=(jax.ShapeDtypeStruct((2, 5, EXT_RO...  39.8 us
    pallas_call x1, Pallas kernels, slots(): pl.pallas_call(slots_kernel, out_shape=(jax.ShapeDtypeStruct((2, 5, EXT_R...  6.52 us
    unnamed x13, local copies, waits for them, and re-layouts  5.44 us

profile of v6, /device:TPU:1, one launch (start us, length us, event | category | flops | bytes accessed | tf_op | source)
XLA Modules:
  0.0 141.4 jit_solution(6406684795478860851)
XLA Ops:
  1.3 0.8 copy.11
  2.0 0.1 reshape.15
  2.1 0.1 pad_add_fusion
  2.2 0.0 copy-start
  2.2 1.3 copy-done
  3.5 0.0 copy-start.3
  3.5 1.4 copy-done.3
  4.9 0.0 copy-start.2
  4.9 0.0 copy-start.4
  4.9 39.8 %halo_in.1 = (f32[2,5,656,128]{3,2,1,0:T(8,128)S(1)}, f32[6,256,256]{2,1,0:T(8,128)S(1)}, s32[9,8,128]{2,1,0:T(8,128)S(1)}) custom-call(f32[2,384,384]{2,1,0:T(8,128)S(1)} %copy-done, f32[6,256,256]{2,1,0:T(8,128)S(1)} %bitcast.4, s32[8,128]{1,0:T(8,128)S(1)} %pad.4.meta), custom_call_target="tpu_custom_call" | custom-call | tf_op jit(solution)/shard_map/halo_in/pallas_call | solution.py:200
  44.8 0.0 copy-done.2
  44.8 0.0 copy-done.4
  44.8 0.0 copy-start.1
  44.8 6.5 %slots.1 = (f32[2,5,656,128]{3,2,1,0:T(8,128)S(1)}, f32[384,384]{1,0:T(8,128)S(1)}, f32[5,2,256,128]{3,2,1,0:T(8,128)S(1)}, f32[8,128]{1,0:T(8,128)S(1)}) custom-call(s32[9,8,128]{2,1,0:T(8,128)S(1)} %get-tuple-element.13.where, f32[2,5,656,128]{3,2,1,0:T(8,128)S(1)} %get-tuple-element.14.ext, f32[2,2,256,256]{3,2,1,0:T(8,128)S(1)} %copy-done.2, ...), custom_call_target="tpu_custom_call" | custom-call | tf_op jit(solution)/shard_map/slots/pallas_call | solution.py:499
  51.3 0.0 copy-done.1
  51.3 87.4 %sums.1 = (f32[2,384,384]{2,1,0:T(8,128)S(1)}, f32[2,2,256,256]{3,2,1,0:T(8,128)S(1)}, f32[8,128]{1,0:T(8,128)S(1)}) custom-call(f32[2,5,656,128]{3,2,1,0:T(8,128)S(1)} %get-tuple-element.16.grad, f32[384,384]{1,0:T(8,128)S(1)} %get-tuple-element.17.weight, f32[2,384,384]{2,1,0:T(8,128)S(1)} %copy-done.1, f32[2,2,256,256]{3,2,1,0:T(8,128)S(1)} %copy-done.2, ...), custom_call_target="tpu_custom_call" | custom-call | tf_op jit(solution)/shard_map/sums/pallas_call | solution.py:801
  138.7 0.6 copy.12
  139.4 1.0 copy.16
  140.4 1.0 copy.17
  (1 shorter events, 0.0 us)
Async XLA Ops:
  2.2 1.3 copy-start
  3.5 1.4 copy-start.3
  4.9 39.9 %copy-start.2 = (f32[2,2,256,256]{3,2,1,0:T(8,128)S(1)}, f32[2,2,256,256]{3,2,1,0:T(8,128)}, u32[]{:S(2)}) copy-start(f32[2,2,256,256]{3,2,1,0:T(8,128)} %probe.3) | copy-start | bytes 3145732
  4.9 39.9 %copy-start.4 = (bf16[8,256,256]{2,1,0:T(8,128)(2,1)S(1)}, bf16[8,256,256]{2,1,0:T(8,128)(2,1)}, u32[]{:S(2)}) copy-start(bf16[8,256,256]{2,1,0:T(8,128)(2,1)} %constant.4.clone.tables_far) | copy-start | bytes 3145732
  44.8 6.5 %copy-start.1 = (f32[2,384,384]{2,1,0:T(8,128)S(1)}, f32[2,384,384]{2,1,0:T(8,128)}, u32[]{:S(2)}) copy-start(f32[2,384,384]{2,1,0:T(8,128)} %obj.3) | copy-start | bytes 3538948

commit v7 on v6

--- a/solution.py
+++ b/solution.py
@@ -558,6 +558,7 @@
     corner_in,
     row_out,
     row_in,
+    middle_in,
     side_out,
     side_in,
     mine,
@@ -608,13 +609,6 @@
     col_ok = [c > 0, c < n_col - 1]
     outer_ok = jnp.where(core == 0, r, n_row - 1 - r) > 0
 
-    half = SHARDS // 2
-    to_mate = send(
-        mine.at[pl.ds(half * (1 - core), half)], mate_part, csend.at[0], crecv.at[0], mate
-    )
-    rows_to_mate = send(
-        grad.at[:, :, pl.ds(inner_from, 128), :], mate_rows, csend.at[2], crecv.at[2], mate
-    )
     edge = pl.ds(outer_from, 128)
     has_left, has_right = col_ok
     far_left, far_right = lax.rem(c, 4) == 0, lax.rem(c, 4) == 3
@@ -628,9 +622,18 @@
     when(has_left & jnp.logical_not(far_left), corner_l.start)
     when(has_right & far_right & outer_ok, jump_r.start)
     when(has_left & far_left & outer_ok, jump_l.start)
+    middle = make(grad.at[:, 2, edge, :], middle_in, hsend.at[7], hrecv.at[7], beyond)
+    when(outer_ok, middle.start)
     corner_left = has_left & (jnp.logical_not(far_left) | outer_ok)
     corner_right = has_right & (jnp.logical_not(far_right) | outer_ok)
     jumped = [has_left & far_left & outer_ok, has_right & far_right & outer_ok]
+    half = SHARDS // 2
+    to_mate = send(
+        mine.at[pl.ds(half * (1 - core), half)], mate_part, csend.at[0], crecv.at[0], mate
+    )
+    rows_to_mate = send(
+        grad.at[:, :, pl.ds(inner_from, 128), :], mate_rows, csend.at[2], crecv.at[2], mate
+    )
 
     rows_to_mate.wait()
     def fill_sides(ch):
@@ -663,13 +666,9 @@
     finish_copy(corner_r, corner_right, corner_left)
     finish_copy(corner_l, corner_left, corner_right)
     for ch in range(2):
-        for t in range(3):
-            v = grad[ch, 1 + t, edge, :]
-            if t == 0:
-                v = v + jnp.where(has_left & jnp.logical_not(far_left), corner_in[0, ch], 0.0)
-            if t == 2:
-                v = v + jnp.where(has_right & jnp.logical_not(far_right), corner_in[1, ch], 0.0)
-            row_out[ch, t] = v
+        for k in range(2):
+            inside = (has_left & jnp.logical_not(far_left), has_right & jnp.logical_not(far_right))[k]
+            row_out[k, ch] = grad[ch, 1 + 2 * k, edge, :] + jnp.where(inside, corner_in[k, ch], 0.0)
     strip = make(row_out, row_in, hsend.at[6], hrecv.at[6], beyond)
     when(outer_ok, strip.start)
     for copy in copies:
@@ -764,35 +763,37 @@
     mean = jnp.sum(sums, axis=0, keepdims=True) / count
     step[...] = jnp.where(rows8.astype(f32) < mine_count, raw[...] - mean, 0.0)
 
-    for ch in range(2):
-        finish_copy(sides[ch][0], has_right, has_left)
-        finish_copy(sides[ch][1], has_left, has_right)
-    for band, start in ((1, 128), (2, inner_to), (0, outer_to)):
-        if band == 0:
-            finish_copy(strip, outer_ok, outer_ok)
-
-        def update(i, _, band=band, start=start):
-            rows = pl.ds(pl.multiple_of(start + i * 8, 8), 8)
-            thin = pl.ds(pl.multiple_of(i * 8, 8), 8)
-            for t in range(3):
-                cols = slice(128 * t, 128 * (t + 1))
-                down = weight[rows, cols] + floor
-                for ch in range(2):
-                    g = grad[ch, 1 + t, pl.ds(pl.multiple_of(136 + start + i * 8, 8), 8), :]
-                    if band == 0:
-                        g = g + jnp.where(outer_ok, row_in[ch, t, thin, :], 0.0)
+    finish_copy(middle, outer_ok, outer_ok)
+    finish_copy(strip, outer_ok, outer_ok)
+    for tiles in ((1,), (0, 2)):
+        if 0 in tiles:
+            for ch in range(2):
+                finish_copy(sides[ch][0], has_right, has_left)
+                finish_copy(sides[ch][1], has_left, has_right)
+        for band, start in ((1, 128), (2, inner_to), (0, outer_to)):
+
+            def update(i, _, band=band, start=start, tiles=tiles):
+                rows = pl.ds(pl.multiple_of(start + i * 8, 8), 8)
+                thin = pl.ds(pl.multiple_of(i * 8, 8), 8)
+                for t in tiles:
+                    k = t // 2
+                    cols = slice(128 * t, 128 * (t + 1))
+                    down = weight[rows, cols] + floor
+                    for ch in range(2):
+                        g = grad[ch, 1 + t, pl.ds(pl.multiple_of(136 + start + i * 8, 8), 8), :]
+                        if band == 0:
+                            v = middle_in[ch, thin, :] if t == 1 else row_in[k, ch, thin, :]
+                            g = g + jnp.where(outer_ok, v, 0.0)
+                            if t != 1:
+                                g = g + jnp.where(jumped[k], corner_in[k, ch, thin, :], 0.0)
+                        if band == 2:
+                            g = g + mate_rows[ch, 1 + t, thin, :]
                         if t != 1:
-                            g = g + jnp.where(jumped[t // 2], corner_in[t // 2, ch, thin, :], 0.0)
-                    if band == 2:
-                        g = g + mate_rows[ch, 1 + t, thin, :]
-                    if t == 0:
-                        g = g + jnp.where(col_ok[0], side_in[0, ch, rows, :], 0.0)
-                    if t == 2:
-                        g = g + jnp.where(col_ok[1], side_in[1, ch, rows, :], 0.0)
-                    obj_new[ch, rows, cols] = obj[ch, rows, cols] + g / down
-            return 0
-
-        lax.fori_loop(0, 16, update, 0, unroll=2)
+                            g = g + jnp.where(col_ok[k], side_in[k, ch, rows, :], 0.0)
+                        obj_new[ch, rows, cols] = obj[ch, rows, cols] + g / down
+                return 0
+
+            lax.fori_loop(0, 16, update, 0, unroll=2)
 
 
 def sums(grad, weight, obj, probe, part, raw):
@@ -810,8 +811,9 @@
         scratch_shapes=[
             VMEM((2, 5, 128, 128), f32),
             VMEM((2, 2, 128, 128), f32),
-            VMEM((2, 3, 128, 128), f32),
-            VMEM((2, 3, 128, 128), f32),
+            VMEM((2, 2, 128, 128), f32),
+            VMEM((2, 2, 128, 128), f32),
+            VMEM((2, 128, 128), f32),
             VMEM((2, 2, TILE, 128), f32),
             VMEM((2, 2, TILE, 128), f32),
             VMEM((SHARDS, PIECE, 128), f32),
@@ -822,8 +824,8 @@
             VMEM((128, 128), f32),
             VMEM((SHARDS, PIECE, 128), f32),
             VMEM((SHARDS * SHARD, 128), f32),
-            dma((7,)),
-            dma((7,)),
+            dma((8,)),
+            dma((8,)),
             dma((3,)),
             dma((3,)),
             dma((30,)),

time: 142 us -> 141 us (level)
    pallas_call x1, Pallas kernels: 6.52 us -> 22.5 us  [slots(): pl.pallas_call(slots_kernel, out_shape=(jax.ShapeDtypeStruct((2, 5, EXT_R...]
    pallas_call x1, Pallas kernels: 87.4 us -> 71.8 us  [sums(): pl.pallas_call(sums_kernel, out_shape=(jax.ShapeDtypeStruct((2, TILE, TIL...]
where the time goes in v7:
time: 141 us; the launch traced here: 142 us
  Pallas kernels  134 us (95%)
  local copies, waits for them, and re-layouts  6.18 us (4%)
    pallas_call x1, Pallas kernels, sums(): pl.pallas_call(sums_kernel, out_shape=(jax.ShapeDtypeStruct((2, TILE, TIL...  71.8 us
    pallas_call x1, Pallas kernels, halo(): pl.pallas_call(halo_kernel, out_shape=(jax.ShapeDtypeStruct((2, 5, EXT_RO...  39.8 us
    pallas_call x1, Pallas kernels, slots(): pl.pallas_call(slots_kernel, out_shape=(jax.ShapeDtypeStruct((2, 5, EXT_R...  22.5 us
    unnamed x13, local copies, waits for them, and re-layouts  5.44 us

profile of v7, /device:TPU:1, one launch (start us, length us, event | category | flops | bytes accessed | tf_op | source)
XLA Modules:
  0.0 141.7 jit_solution(1654847784547331542)
XLA Ops:
  1.3 0.8 copy.11
  2.0 0.1 reshape.15
  2.1 0.1 pad_add_fusion
  2.2 0.0 copy-start
  2.2 1.3 copy-done
  3.5 0.0 copy-start.3
  3.5 1.4 copy-done.3
  4.9 0.0 copy-start.2
  4.9 0.0 copy-start.4
  4.9 39.8 %halo_in.1 = (f32[2,5,656,128]{3,2,1,0:T(8,128)S(1)}, f32[6,256,256]{2,1,0:T(8,128)S(1)}, s32[9,8,128]{2,1,0:T(8,128)S(1)}) custom-call(f32[2,384,384]{2,1,0:T(8,128)S(1)} %copy-done, f32[6,256,256]{2,1,0:T(8,128)S(1)} %bitcast.4, s32[8,128]{1,0:T(8,128)S(1)} %pad.4.meta), custom_call_target="tpu_custom_call" | custom-call | tf_op jit(solution)/shard_map/halo_in/pallas_call | solution.py:200
  44.8 0.0 copy-done.2
  44.8 0.0 copy-done.4
  44.8 0.0 copy-start.1
  44.8 22.5 %slots.1 = (f32[2,5,656,128]{3,2,1,0:T(8,128)S(1)}, f32[384,384]{1,0:T(8,128)S(1)}, f32[5,2,256,128]{3,2,1,0:T(8,128)S(1)}, f32[8,128]{1,0:T(8,128)S(1)}) custom-call(s32[9,8,128]{2,1,0:T(8,128)S(1)} %get-tuple-element.13.where, f32[2,5,656,128]{3,2,1,0:T(8,128)S(1)} %get-tuple-element.14.ext, f32[2,2,256,256]{3,2,1,0:T(8,128)S(1)} %copy-done.2, ...), custom_call_target="tpu_custom_call" | custom-call | tf_op jit(solution)/shard_map/slots/pallas_call | solution.py:499
  67.3 0.0 copy-done.1
  67.3 71.8 %sums.1 = (f32[2,384,384]{2,1,0:T(8,128)S(1)}, f32[2,2,256,256]{3,2,1,0:T(8,128)S(1)}, f32[8,128]{1,0:T(8,128)S(1)}) custom-call(f32[2,5,656,128]{3,2,1,0:T(8,128)S(1)} %get-tuple-element.16.grad, f32[384,384]{1,0:T(8,128)S(1)} %get-tuple-element.17.weight, f32[2,384,384]{2,1,0:T(8,128)S(1)} %copy-done.1, f32[2,2,256,256]{3,2,1,0:T(8,128)S(1)} %copy-done.2, ...), custom_call_target="tpu_custom_call" | custom-call | tf_op jit(solution)/shard_map/sums/pallas_call | solution.py:802
  139.1 0.6 copy.12
  139.7 1.0 copy.16
  140.7 1.0 copy.17
  (1 shorter events, 0.0 us)
Async XLA Ops:
  2.2 1.3 copy-start
  3.5 1.4 copy-start.3
  4.9 39.9 %copy-start.2 = (f32[2,2,256,256]{3,2,1,0:T(8,128)S(1)}, f32[2,2,256,256]{3,2,1,0:T(8,128)}, u32[]{:S(2)}) copy-start(f32[2,2,256,256]{3,2,1,0:T(8,128)} %probe.3) | copy-start | bytes 3145732
  4.9 39.9 %copy-start.4 = (bf16[8,256,256]{2,1,0:T(8,128)(2,1)S(1)}, bf16[8,256,256]{2,1,0:T(8,128)(2,1)}, u32[]{:S(2)}) copy-start(bf16[8,256,256]{2,1,0:T(8,128)(2,1)} %constant.4.clone.tables_far) | copy-start | bytes 3145732
  44.8 22.5 %copy-start.1 = (f32[2,384,384]{2,1,0:T(8,128)S(1)}, f32[2,384,384]{2,1,0:T(8,128)}, u32[]{:S(2)}) copy-start(f32[2,384,384]{2,1,0:T(8,128)} %obj.3) | copy-start | bytes 3538948
